TPU v7x, 1024 devices: a whole 4x4x32 slice. The times are simulated.
1024 devices in a mesh: inner: 16 (over y, z_hi, core), outer: 64 (over x, z_lo).
Axes of the slice: x: 4, y: 4, z: 32 (z_hi: 2, z_lo: 16; z = z_hi * 16 + z_lo), core: 2. Of those that a mesh axis runs over, the one named last changes fastest.
Arguments:
- tokens: bfloat16 [2048, 4096], P('inner'), may hold values from -6 to 6
- weight_codes: bfloat16 [2, 4096, 11008], P(None, 'inner', 'outer'), may hold values from -1 to 1
- block_scales: float32 [2, 2, 11008], P(None, None, 'outer'), may hold values from 0.01 to 0.08
- grad_hidden: bfloat16 [2048, 11008], P('inner', 'outer'), may hold values from -6 to 6
Outputs:
- hidden: bfloat16 [2048, 11008], P('inner', 'outer')
- token_grads: float32 [2048, 4096], P('inner', 'outer')
- weight_grads: float32 [2, 4096, 11008], P(None, 'inner', 'outer')
All inputs are finite; a program needn't handle non-finite values.
Results may differ from a plain program's by a relative error of at most 0.015.
Values may be sent and summed in bfloat16 or wider, within the bound.
A program may use at most 64 MiB of HBM per device.

v0:
```python
import math

import jax
import jax.numpy as jnp
from jax import lax
from jax.sharding import PartitionSpec as P


def dequantize(codes, scales):
    block_count = scales.shape[1]
    shaped = codes.reshape(2, block_count, codes.shape[1] // block_count, codes.shape[2])
    values = shaped.astype(jnp.float32) * scales[:, :, None, :]
    return values.reshape(codes.shape).astype(jnp.bfloat16)


def local(tokens, weight_codes, block_scales, grad_hidden):
    rows_dev = tokens.shape[0]
    model_width = tokens.shape[1]
    units = weight_codes.shape[2]
    group_size = lax.axis_size("inner")
    all_codes = lax.all_gather(weight_codes, "inner", axis=1, tiled=True)
    weights = dequantize(all_codes, block_scales)
    gate = jnp.dot(tokens, weights[0], preferred_element_type=jnp.float32)
    up_proj = jnp.dot(tokens, weights[1], preferred_element_type=jnp.float32)
    sigmoid_gate = jax.nn.sigmoid(gate)
    hidden = (gate * sigmoid_gate * up_proj).astype(jnp.bfloat16)
    cotangent = grad_hidden.astype(jnp.float32)
    d_gate = (cotangent * up_proj * sigmoid_gate * (1.0 + gate * (1.0 - sigmoid_gate))).astype(
        jnp.bfloat16
    )
    d_up = (cotangent * gate * sigmoid_gate).astype(jnp.bfloat16)
    term = lax.dot_general(
        d_gate, weights[0], (((1,), (1,)), ((), ())), preferred_element_type=jnp.float32
    )
    term = term + lax.dot_general(
        d_up, weights[1], (((1,), (1,)), ((), ())), preferred_element_type=jnp.float32
    )
    token_grads = lax.psum_scatter(term, "outer", scatter_dimension=1, tiled=True)
    left_side = jnp.concatenate([d_gate, d_up], axis=1)
    row_count = model_width // group_size
    joined = lax.dot_general(
        tokens, left_side, (((0,), (0,)), ((), ())), preferred_element_type=jnp.float32
    )
    grad_rows = lax.psum_scatter(
        lax.optimization_barrier(joined.astype(jnp.bfloat16))
        .astype(jnp.float32)
        .astype(jnp.bfloat16),
        "inner",
        scatter_dimension=0,
        tiled=True,
    ).astype(jnp.float32)
    total_tokens = rows_dev * group_size
    weight_grads = grad_rows.reshape(row_count, 2, units).transpose(1, 0, 2) * (
        1.0 / math.sqrt(total_tokens)
    )
    return (hidden, token_grads, weight_grads)


def solution(mesh):
    return jax.shard_map(
        local,
        mesh=mesh,
        in_specs=(
            P("inner", None),
            P(None, "inner", "outer"),
            P(None, None, "outer"),
            P("inner", "outer"),
        ),
        out_specs=(P("inner", "outer"), P("inner", "outer"), P(None, "inner", "outer")),
        check_vma=False,
    )
```

profile of v0, /device:TPU:16, one launch (start us, length us, event | category | flops | bytes accessed | tf_op | source)
XLA Modules:
  0.0 1173.3 jit_solution(1798587435451510957)
XLA Ops:
  7.2 0.0 copy-start
  7.2 0.0 all-gather.2.cloned.1.call-start
  7.2 1.7 copy.12
  8.9 0.0 all-gather.2.cloned.1.call-update
  8.9 0.0 reduce-scatter.5.cloned.1.call-start
  9.0 0.8 copy.13
  9.8 4.1 mul.47
  13.9 8.2 mul.48
  22.1 0.0 copy-start.3
  22.1 167.9 %all-gather.2.cloned.1.call-done = bf16[2,4096,172]{1,2,0:T(8,128)(2,1)} async-done(((bf16[2,256,172]{1,2,0:T(8,128)(2,1)}), bf16[2,4096,172]{1,2,0:T(8,128)(2,1)}) %all-gather.2.cloned.1.call-update) | async-done | bytes 2818064 | tf_op jit(solution)/shard_map/all_gather | solution.py:21
  190.0 4.4 multiply_convert_fusion
  194.4 0.0 copy-done
  194.4 0.0 copy-start.1
  194.4 0.5 fusion.5
  194.9 0.0 copy-done.3
  194.9 1.2 fusion.8
  196.1 0.0 copy-done.1
  196.1 2.5 fusion
  198.6 0.0 reduce-scatter.5.cloned.1.call-update
  198.6 0.0 reduce-scatter.3.cloned.1.call-start
  198.7 0.0 copy-start.2
  198.7 2.5 fusion.1
  201.2 0.0 copy-done.2
  201.2 2.3 convolution_add_fusion
  203.5 0.0 reduce-scatter.3.cloned.1.call-update
  203.5 189.9 %reduce-scatter.5.cloned.1.call-done = bf16[256,344]{0,1:T(8,128)(2,1)} async-done(((bf16[4096,344]{0,1:T(8,128)(2,1)}), bf16[256,344]{0,1:T(8,128)(2,1)}) %reduce-scatter.5.cloned.1.call-update) | async-done | bytes 176144 | tf_op jit(solution)/shard_map/reduce_scatter | solution.py:44
  393.4 0.9 convert_multiply_fusion
  394.4 1.0 copy.14
  395.4 771.4 %reduce-scatter.3.cloned.1.call-done = f32[128,64]{0,1:T(8,128)} async-done(((f32[128,4096]{0,1:T(8,128)}), f32[128,64]{0,1:T(8,128)}) %reduce-scatter.3.cloned.1.call-update) | async-done | bytes 32784 | tf_op jit(solution)/shard_map/reduce_scatter | solution.py:38
  (1 shorter events, 0.0 us)
Async XLA Ops:
  7.2 187.2 %copy-start = (bf16[128,4096]{1,0:T(8,128)(2,1)S(1)}, bf16[128,4096]{1,0:T(8,128)(2,1)}, u32[]{:S(2)}) copy-start(bf16[128,4096]{1,0:T(8,128)(2,1)} %param.4) | copy-start | bytes 3145732
  7.2 182.8 %all-gather.2.cloned.1.call-start = ((), (), s32[]{:S(2)}) async-start(), calls=%async_computation.2 | async-start | bytes 3063808 | tf_op jit(solution)/shard_map/all_gather | solution.py:21
  8.9 384.5 %reduce-scatter.5.cloned.1.call-start = ((), (), s32[]{:S(2)}) async-start(), calls=%async_computation.4 | async-start | bytes 2994176 | tf_op jit(solution)/shard_map/reduce_scatter | solution.py:44
  22.1 172.8 %copy-start.3 = (bf16[128,172]{0,1:T(8,128)(2,1)S(1)}, bf16[128,172]{0,1:T(8,128)(2,1)}, u32[]{:S(2)}) copy-start(bf16[128,172]{0,1:T(8,128)(2,1)} %param.7) | copy-start | bytes 132100
  194.4 1.7 copy-start.1
  198.6 968.2 %reduce-scatter.3.cloned.1.call-start = ((), (), s32[]{:S(2)}) async-start(), calls=%async_computation.3 | async-start | bytes 2129920 | tf_op jit(solution)/shard_map/reduce_scatter | solution.py:38
  198.7 2.5 copy-start.2
Sparse Core Ops, SparseCore 0:
  12.9 177.0 all-gather.1
  198.7 194.6 reduce-scatter.4
  397.8 769.0 reduce-scatter.2
where the time goes:
time: 1170 us
  waiting for transfers between devices  1130 us (97%)
  local copies, waits for them, and re-layouts  15.9 us (1%)
  between operations  13.8 us (1%)
    reduce_scatter x1, waiting for transfers between devices, local(): lax.psum_scatter(term, 'outer', scatter_dimension=1, tiled=True)  771 us
    reduce_scatter x1, waiting for transfers between devices, local(): lax.psum_scatter(lax.optimization_barrier(joined.astype(jnp.bfloat16)).as...  190 us
    all_gather x1, waiting for transfers between devices, local(): all_codes = lax.all_gather(weight_codes, 'inner', axis=1, tiled=True)  168 us
  transfers between devices with their start and end apart: 3, of which 3 were waited for; matrix products, arithmetic and copies ran while one was open for 2% of the time, Pallas kernels for 0%

commit v1 on v0

v1 whole, which is shorter than its diff:
```python
import math

import jax
import jax.numpy as jnp
from jax import lax
from jax.experimental import pallas as pl
from jax.experimental.pallas import tpu as pltpu
from jax.sharding import PartitionSpec as P

MESH = pl.DeviceIdType.MESH
BLOCK = 2048
F32 = jnp.float32
BF16 = jnp.bfloat16

NY, NX, NA, NB, NZ = 4, 4, 4, 4, 16
HALF = 176
ROWS = 2 * HALF
COLS = 256
TOK = 128
CHUNKS = ((0, 96), (96, 96), (192, 96), (288, 64))
NCH = len(CHUNKS)


def dot(a, b):
    return lax.dot_general(a, b, (((1,), (0,)), ((), ())), preferred_element_type=F32)


def dot_nt(a, b):
    return lax.dot_general(a, b, (((1,), (1,)), ((), ())), preferred_element_type=F32)


def kernel(
    wt_ref, tok_ref, gh_ref, hid_ref, tg_ref, wg_ref,
    w_all, acc, d_t, d_f, d_b,
    x_out, x_in, r_out, r_in, s_out, s_in,
    c_out, c_in, own, y_out, y_in, z_out, z_in,
    fz_s, fz_r, fy_s, fy_r, fc_s, fc_r,
    bc_s, bc_r, by_s, by_r, bz_s, bz_r,
    cx_s, cx_r, cr_s, cr_r, cs_s, cs_r,
):
    me = lax.axis_index("inner")
    ou = lax.axis_index("outer")
    y, zh, c = me // 4, (me // 2) % 2, me % 2
    x, zl = ou // NZ, ou % NZ
    a, b = zl // NB, zl % NB

    def inner(yy, zz, cc):
        return yy * 4 + zz * 2 + cc

    z_dev = {"inner": inner(y, 1 - zh, c)}
    c_dev = {"inner": inner(y, zh, 1 - c)}
    y_dev = [{"inner": inner((y + d) % NY, zh, c)} for d in range(NY)]
    x_dev = [{"outer": ((x + d) % NX) * NZ + zl} for d in range(NX)]
    r_dev = [{"outer": x * NZ + a * NB + (b + d) % NB} for d in range(NB)]
    s_dev = [{"outer": x * NZ + ((a + d) % NA) * NB + b} for d in range(NA)]

    sent = []

    def send(src, dst, s_sem, r_sem, device):
        copy = pltpu.make_async_remote_copy(
            src_ref=src, dst_ref=dst, send_sem=s_sem, recv_sem=r_sem,
            device_id=device, device_id_type=MESH,
        )
        copy.start()
        sent.append(copy)
        return copy

    barrier = pltpu.get_barrier_semaphore()
    peers = [z_dev] + s_dev[1:] + x_dev[1:] + y_dev[1:] + r_dev[1:] + [c_dev]
    for device in peers:
        pl.semaphore_signal(barrier, inc=1, device_id=device, device_id_type=MESH)
    w_all[me] = wt_ref[...]
    acc[...] = jnp.zeros_like(acc)
    pl.semaphore_wait(barrier, len(peers))

    with jax.named_scope("gather_weights"):
        fz, fy, fc = {}, {}, {}
        for k, (at, n) in enumerate(CHUNKS):
            part = w_all.at[me, pl.ds(at, n)]
            fz[k] = send(part, part, fz_s.at[k], fz_r.at[k], z_dev)
        mine = w_all.at[me]
        for d in (1, 3, 2):
            fy[d, 0] = send(mine, mine, fy_s.at[d, 0], fy_r.at[d, 0], y_dev[d])
        fc[0, 0] = send(mine, mine, fc_s.at[0, 0], fc_r.at[0, 0], c_dev)

        def tok_cols(j):
            return tok_ref[:, pl.ds(pl.multiple_of(j * COLS, COLS), COLS)]

        for d in (1, 3, 2):
            fy[d, 0].wait_recv()
            block = w_all.at[inner((y - d + NY) % NY, zh, c)]
            fc[d, 0] = send(block, block, fc_s.at[d, 0], fc_r.at[d, 0], c_dev)
        for d in range(NY):
            fc[d, 0].wait_recv()

        def add_blocks(side, at, n):
            def step(t, _):
                j = inner(t // 2, side, t % 2)
                acc[pl.ds(at, n), :] += dot_nt(w_all[j, pl.ds(at, n), :], tok_cols(j))
                return 0

            lax.fori_loop(0, 2 * NY, step, 0)

        add_blocks(zh, 0, ROWS)

        def pass_on(k):
            at, n = CHUNKS[k]
            for d in (1, 3, 2):
                fy[d, 1 + k].wait_recv()
                part = w_all.at[inner((y - d + NY) % NY, 1 - zh, c), pl.ds(at, n)]
                fc[d, 1 + k] = send(part, part, fc_s.at[d, 1 + k], fc_r.at[d, 1 + k], c_dev)

        def use(k):
            at, n = CHUNKS[k]
            for d in range(NY):
                fc[d, 1 + k].wait_recv()
            add_blocks(1 - zh, at, n)

        for k, (at, n) in enumerate(CHUNKS):
            fz[k].wait_recv()
            part = w_all.at[inner(y, 1 - zh, c), pl.ds(at, n)]
            for d in (1, 3, 2):
                fy[d, 1 + k] = send(part, part, fy_s.at[d, 1 + k], fy_r.at[d, 1 + k], y_dev[d])
            fc[0, 1 + k] = send(part, part, fc_s.at[0, 1 + k], fc_r.at[0, 1 + k], c_dev)
            if k > 0:
                pass_on(k - 1)
                use(k - 1)
        pass_on(NCH - 1)
        use(NCH - 1)

    with jax.named_scope("activations"):
        gate = acc[:HALF, :]
        up = acc[HALF:, :]
        sig = jax.nn.sigmoid(gate)
        silu = gate * sig
        hid_ref[...] = (silu * up).astype(BF16)
        cot = gh_ref[...].astype(F32)
        d_gate = (cot * up * sig * (1.0 + gate * (1.0 - sig))).astype(BF16)
        d_up = (cot * silu).astype(BF16)
        d_t[:HALF, :] = d_gate
        d_t[HALF:, :] = d_up
        d_f[:HALF, :] = d_gate.astype(F32)
        d_f[HALF:ROWS, :] = d_up.astype(F32)
        d_f[ROWS:, :] = jnp.zeros((d_f.shape[0] - ROWS, TOK), F32)
        d_b[...] = d_f[...].T.astype(BF16)

    bc, by, bz = {}, {}, {}

    def weight_part(j):
        return dot(d_t[...], tok_cols(j))

    def to_core(e):
        side = 1 - zh if e == 0 else zh
        for d in (1, 3, 2, 0):
            s = 2 * d + e
            c_out[s] = weight_part(inner((y + d) % NY, side, 1 - c)).astype(BF16)
            bc[s] = send(c_out.at[s], c_in.at[s], bc_s.at[s], bc_r.at[s], c_dev)

    def to_y(e):
        side = 1 - zh if e == 0 else zh
        for d in (1, 3, 2, 0):
            s = 2 * d + e
            part = weight_part(inner((y + d) % NY, side, c))
            bc[s].wait_recv()
            total = part + c_in[s].astype(F32)
            if d == 0:
                own[e] = total
                continue
            y_out[d - 1, e] = total.astype(BF16)
            cuts = CHUNKS if e == 0 else ((0, ROWS),)
            for k, (at, n) in enumerate(cuts):
                slot = k if e == 0 else NCH
                by[d, e, k] = send(
                    y_out.at[d - 1, e, pl.ds(at, n)], y_in.at[d - 1, e, pl.ds(at, n)],
                    by_s.at[d - 1, slot], by_r.at[d - 1, slot], y_dev[d],
                )

    with jax.named_scope("weight_grads_far"):
        to_core(0)
        to_y(0)

    cx, cr, cs = {}, {}, {}
    with jax.named_scope("token_grads_x"):
        for d in (1, 3, 2, 0):
            xb = (x + d) % NX

            def step(q, _, xb=xb):
                x_out[xb, q] = dot(d_b[:, :ROWS], w_all[4 * xb + q]).astype(BF16)
                return 0

            lax.fori_loop(0, 4, step, 0)
            if d > 0:
                cx[d] = send(
                    x_out.at[xb], x_in.at[d - 1], cx_s.at[d - 1], cx_r.at[d - 1], x_dev[d]
                )

    with jax.named_scope("weight_grads_z"):
        for k, (at, n) in enumerate(CHUNKS):
            rows = pl.ds(at, n)
            total = own[0, rows, :]
            for d in (1, 3, 2):
                by[d, 0, k].wait_recv()
                total = total + y_in[d - 1, 0, rows, :].astype(F32)
            z_out[rows, :] = total.astype(BF16)
            bz[k] = send(
                z_out.at[rows], z_in.at[rows], bz_s.at[k], bz_r.at[k], z_dev
            )

    with jax.named_scope("weight_grads_near"):
        to_core(1)
        to_y(1)

    lane = lax.broadcasted_iota(jnp.int32, (TOK, 128), 1)
    low = lane < 64
    with jax.named_scope("token_grads_run"):
        for d in (1, 3, 2):
            cx[d].wait_recv()

        def x_total(q, h):
            cols = pl.ds(128 * h, 128)
            total = x_out[x, q, :, cols].astype(F32)
            for d in (1, 2, 3):
                total = total + x_in[d - 1, q, :, cols].astype(F32)
            return total

        for h in range(2):
            for m in range(2):
                even, odd = x_total(2 * m, h), x_total(2 * m + 1, h)
                r_out[2 * h, m] = jnp.where(low, even, pltpu.roll(odd, 64, 1)).astype(BF16)
                r_out[2 * h + 1, m] = jnp.where(low, pltpu.roll(even, 64, 1), odd).astype(BF16)
        for d in (1, 2, 3):
            cr[d] = send(
                r_out.at[(b + d) % NB], r_in.at[d - 1], cr_s.at[d - 1], cr_r.at[d - 1], r_dev[d]
            )

    with jax.named_scope("weight_grads_own"):
        for d in (1, 3, 2):
            by[d, 1, 0].wait_recv()
        for at, n in CHUNKS:
            rows = pl.ds(at, n)
            total = own[1, rows, :]
            for d in (1, 2, 3):
                total = total + y_in[d - 1, 1, rows, :].astype(F32)
            own[1, rows, :] = total

    with jax.named_scope("token_grads_strided"):
        for d in (1, 2, 3):
            cr[d].wait_recv()
        for m in range(2):
            total = r_out[b, m].astype(F32)
            for d in (1, 2, 3):
                total = total + r_in[d - 1, m].astype(F32)
            turned = pltpu.roll(total, 64, 1)
            s_out[2 * m] = jnp.where(low[:64], total[:64], turned[64:]).astype(BF16)
            s_out[2 * m + 1] = jnp.where(low[:64], turned[:64], total[64:]).astype(BF16)
        for d in (1, 2, 3):
            cs[d] = send(
                s_out.at[(a + d) % NA], s_in.at[d - 1], cs_s.at[d - 1], cs_r.at[d - 1], s_dev[d]
            )
        for d in (1, 2, 3):
            cs[d].wait_recv()
        total = s_out[a].astype(F32)
        for d in (1, 2, 3):
            total = total + s_in[d - 1].astype(F32)
        tg_ref[:64, :] = total[:, :64]
        tg_ref[64:, :] = pltpu.roll(total, 64, 1)[:, :64]

    with jax.named_scope("weight_grads_last"):
        factor = 1.0 / math.sqrt(16 * TOK)
        for k, (at, n) in enumerate(CHUNKS):
            rows = pl.ds(at, n)
            bz[k].wait_recv()
            wg_ref[rows, :] = (own[1, rows, :] + z_in[rows, :].astype(F32)) * factor

    for copy in sent:
        copy.wait_send()


def local(tokens, weight_codes, block_scales, grad_hidden):
    units = weight_codes.shape[2]
    me = lax.axis_index("inner")
    block = me * COLS // BLOCK
    scales = lax.dynamic_index_in_dim(block_scales, block, 1, keepdims=True)
    weights = (weight_codes.astype(F32) * scales).astype(BF16)
    pad = HALF - units
    wt = jnp.pad(weights.transpose(0, 2, 1), ((0, 0), (0, pad), (0, 0))).reshape(ROWS, COLS)
    gh = jnp.pad(grad_hidden.T, ((0, pad), (0, 0)))
    dma = pltpu.SemaphoreType.DMA
    vmem = pl.BlockSpec(memory_space=pltpu.VMEM)
    hidden_t, token_grads, grads_t = pl.pallas_call(
        kernel,
        out_shape=(
            jax.ShapeDtypeStruct((HALF, TOK), BF16),
            jax.ShapeDtypeStruct((TOK, 64), F32),
            jax.ShapeDtypeStruct((ROWS, COLS), F32),
        ),
        in_specs=[vmem] * 3,
        out_specs=(vmem,) * 3,
        scratch_shapes=[
            pltpu.VMEM((16, ROWS, COLS), BF16),
            pltpu.VMEM((ROWS, TOK), F32),
            pltpu.VMEM((ROWS, TOK), BF16),
            pltpu.VMEM((384, TOK), F32),
            pltpu.VMEM((TOK, 384), BF16),
            pltpu.VMEM((NX, 4, TOK, COLS), BF16),
            pltpu.VMEM((NX - 1, 4, TOK, COLS), BF16),
            pltpu.VMEM((NB, 2, TOK, 128), BF16),
            pltpu.VMEM((NB - 1, 2, TOK, 128), BF16),
            pltpu.VMEM((NA, 64, 128), BF16),
            pltpu.VMEM((NA - 1, 64, 128), BF16),
            pltpu.VMEM((8, ROWS, COLS), BF16),
            pltpu.VMEM((8, ROWS, COLS), BF16),
            pltpu.VMEM((2, ROWS, COLS), F32),
            pltpu.VMEM((NY - 1, 2, ROWS, COLS), BF16),
            pltpu.VMEM((NY - 1, 2, ROWS, COLS), BF16),
            pltpu.VMEM((ROWS, COLS), BF16),
            pltpu.VMEM((ROWS, COLS), BF16),
            dma((NCH,)), dma((NCH,)),
            dma((NY, 1 + NCH)), dma((NY, 1 + NCH)),
            dma((NY, 1 + NCH)), dma((NY, 1 + NCH)),
            dma((8,)), dma((8,)),
            dma((NY - 1, 1 + NCH)), dma((NY - 1, 1 + NCH)),
            dma((NCH,)), dma((NCH,)),
            dma((3,)), dma((3,)),
            dma((3,)), dma((3,)),
            dma((3,)), dma((3,)),
        ],
        compiler_params=pltpu.CompilerParams(
            collective_id=0, has_side_effects=True, vmem_limit_bytes=44 * 2**20
        ),
        name="ffn_grads",
    )(wt, tokens, gh)
    hidden = hidden_t[:units].T
    weight_grads = grads_t.reshape(2, HALF, COLS)[:, :units].transpose(0, 2, 1)
    return (hidden, token_grads, weight_grads)


def solution(mesh):
    return jax.shard_map(
        local,
        mesh=mesh,
        in_specs=(
            P("inner", None),
            P(None, "inner", "outer"),
            P(None, None, "outer"),
            P("inner", "outer"),
        ),
        out_specs=(P("inner", "outer"), P("inner", "outer"), P(None, "inner", "outer")),
        check_vma=False,
    )
```

time: 1170 us -> 131 us (0.11)
  the two profiles are of different devices: /device:TPU:16 before, /device:TPU:1 now
where the time goes in v1:
time: 131 us
  Pallas kernels  126 us (96%)
  local copies, waits for them, and re-layouts  3.36 us (3%)
    pallas_call x1, Pallas kernels, local(): pl.pallas_call(kernel, out_shape=(jax.ShapeDtypeStruct((HALF, TOK), BF16)...  126 us

profile of v1, /device:TPU:1, one launch (start us, length us, event | category | flops | bytes accessed | tf_op | source)
XLA Modules:
  0.0 130.8 jit_solution(11390998181260831603)
XLA Ops:
  0.6 0.0 copy-start
  0.6 0.0 copy-start.3
  0.7 0.0 copy-start.2
  0.7 0.0 copy-start.1
  0.7 0.6 copy-done
  1.3 0.1 copy-done.3
  1.4 0.1 copy.14
  1.6 0.0 copy-done.2
  1.6 0.2 fusion
  1.9 0.1 copy-done.1
  2.0 126.5 %ffn_grads.1 = (bf16[176,128]{1,0:T(8,128)(2,1)S(1)}, f32[128,64]{1,0:T(8,128)S(1)}, f32[352,256]{1,0:T(8,128)S(1)}) custom-call(bf16[352,256]{1,0:T(8,128)(2,1)S(1)} %bitcast.12, bf16[128,4096]{1,0:T(8,128)(2,1)S(1)} %copy-done.1, bf16[176,128]{1,0:T(8,128)(2,1)S(1)} %pad.9.gh_ref), custom_call_target="tpu_custom_call" | custom-call | tf_op jit(solution)/shard_map/ffn_grads/pallas_call | solution.py:290
  128.5 0.6 slice_bitcast_fusion
  129.1 0.7 copy.13
  129.8 1.0 copy.18
  (4 shorter events, 0.0 us)
Async XLA Ops:
  0.6 0.7 copy-start
  0.6 0.8 copy-start.3
  0.7 0.9 copy-start.2
  0.7 1.3 %copy-start.1 = (bf16[128,4096]{1,0:T(8,128)(2,1)S(1)}, bf16[128,4096]{1,0:T(8,128)(2,1)}, u32[]{:S(2)}) copy-start(bf16[128,4096]{1,0:T(8,128)(2,1)} %tok_ref.1) | copy-start | bytes 3145732

commit v2 on v1

--- a/solution.py
+++ b/solution.py
@@ -31,12 +31,13 @@
 
 def kernel(
     wt_ref, tok_ref, gh_ref, hid_ref, tg_ref, wg_ref,
-    w_all, acc, d_t, d_f, d_b,
+    w_all, acc, d_t, d_f, d_b, d_in, tok_in,
     x_out, x_in, r_out, r_in, s_out, s_in,
-    c_out, c_in, own, y_out, y_in, z_out, z_in,
+    c_out, c_in, own, y_out, y_in,
     fz_s, fz_r, fy_s, fy_r, fc_s, fc_r,
-    bc_s, bc_r, by_s, by_r, bz_s, bz_r,
+    bz_s, bz_r, bc_s, bc_r, by_s, by_r,
     cx_s, cx_r, cr_s, cr_r, cs_s, cs_r,
+    ta_s, ta_r, ts_s, ts_r, tr_s, tr_r, tx_s, tx_r,
 ):
     me = lax.axis_index("inner")
     ou = lax.axis_index("outer")
@@ -75,6 +76,14 @@
 
     with jax.named_scope("gather_weights"):
         fz, fy, fc = {}, {}, {}
+        shard_rows = pl.ds(pl.multiple_of((b % 2) * 64 + a * 16, 16), 16)
+        shard = 2 * x + b // 2
+        shard_cols = inner(shard // 2, 1 - zh, shard % 2)
+        shard_cols = pl.ds(pl.multiple_of(shard_cols * COLS, COLS), COLS)
+        ta = send(
+            tok_ref.at[shard_rows, shard_cols], tok_in.at[shard, shard_rows],
+            ta_s.at[0], ta_r.at[0], z_dev,
+        )
         for k, (at, n) in enumerate(CHUNKS):
             part = w_all.at[me, pl.ds(at, n)]
             fz[k] = send(part, part, fz_s.at[k], fz_r.at[k], z_dev)
@@ -125,6 +134,11 @@
             if k > 0:
                 pass_on(k - 1)
                 use(k - 1)
+        ta.wait_recv()
+        ts = {}
+        for d in (1, 2, 3):
+            part = tok_in.at[shard, shard_rows]
+            ts[d] = send(part, part, ts_s.at[d - 1], ts_r.at[d - 1], s_dev[d])
         pass_on(NCH - 1)
         use(NCH - 1)
 
@@ -139,117 +153,133 @@
         d_up = (cot * silu).astype(BF16)
         d_t[:HALF, :] = d_gate
         d_t[HALF:, :] = d_up
+        bz = {}
+        for k, (at, n) in enumerate(CHUNKS):
+            rows = pl.ds(at, n)
+            bz[k] = send(d_t.at[rows], d_in.at[rows], bz_s.at[k], bz_r.at[k], z_dev)
         d_f[:HALF, :] = d_gate.astype(F32)
         d_f[HALF:ROWS, :] = d_up.astype(F32)
         d_f[ROWS:, :] = jnp.zeros((d_f.shape[0] - ROWS, TOK), F32)
         d_b[...] = d_f[...].T.astype(BF16)
 
-    bc, by, bz = {}, {}, {}
-
-    def weight_part(j):
-        return dot(d_t[...], tok_cols(j))
-
-    def to_core(e):
-        side = 1 - zh if e == 0 else zh
-        for d in (1, 3, 2, 0):
-            s = 2 * d + e
-            c_out[s] = weight_part(inner((y + d) % NY, side, 1 - c)).astype(BF16)
-            bc[s] = send(c_out.at[s], c_in.at[s], bc_s.at[s], bc_r.at[s], c_dev)
-
-    def to_y(e):
-        side = 1 - zh if e == 0 else zh
-        for d in (1, 3, 2, 0):
-            s = 2 * d + e
-            part = weight_part(inner((y + d) % NY, side, c))
-            bc[s].wait_recv()
-            total = part + c_in[s].astype(F32)
-            if d == 0:
-                own[e] = total
-                continue
-            y_out[d - 1, e] = total.astype(BF16)
-            cuts = CHUNKS if e == 0 else ((0, ROWS),)
-            for k, (at, n) in enumerate(cuts):
-                slot = k if e == 0 else NCH
-                by[d, e, k] = send(
-                    y_out.at[d - 1, e, pl.ds(at, n)], y_in.at[d - 1, e, pl.ds(at, n)],
-                    by_s.at[d - 1, slot], by_r.at[d - 1, slot], y_dev[d],
-                )
-
-    with jax.named_scope("weight_grads_far"):
-        to_core(0)
-        to_y(0)
-
     cx, cr, cs = {}, {}, {}
     with jax.named_scope("token_grads_x"):
-        for d in (1, 3, 2, 0):
-            xb = (x + d) % NX
-
-            def step(q, _, xb=xb):
-                x_out[xb, q] = dot(d_b[:, :ROWS], w_all[4 * xb + q]).astype(BF16)
-                return 0
-
-            lax.fori_loop(0, 4, step, 0)
-            if d > 0:
-                cx[d] = send(
-                    x_out.at[xb], x_in.at[d - 1], cx_s.at[d - 1], cx_r.at[d - 1], x_dev[d]
-                )
-
-    with jax.named_scope("weight_grads_z"):
-        for k, (at, n) in enumerate(CHUNKS):
-            rows = pl.ds(at, n)
-            total = own[0, rows, :]
-            for d in (1, 3, 2):
-                by[d, 0, k].wait_recv()
-                total = total + y_in[d - 1, 0, rows, :].astype(F32)
-            z_out[rows, :] = total.astype(BF16)
-            bz[k] = send(
-                z_out.at[rows], z_in.at[rows], bz_s.at[k], bz_r.at[k], z_dev
-            )
-
-    with jax.named_scope("weight_grads_near"):
-        to_core(1)
-        to_y(1)
+        for m in range(2):
+            for d in (1, 3, 2, 0):
+                xb = (x + d) % NX
+
+                def step(q, _, xb=xb):
+                    x_out[xb, q] = dot(d_b[:, :ROWS], w_all[4 * xb + q]).astype(BF16)
+                    return 0
+
+                lax.fori_loop(2 * m, 2 * m + 2, step, 0)
+                if d > 0:
+                    pair = pl.ds(2 * m, 2)
+                    cx[d, m] = send(
+                        x_out.at[xb, pair], x_in.at[d - 1, pair],
+                        cx_s.at[m, d - 1], cx_r.at[m, d - 1], x_dev[d],
+                    )
+
+    tr, tx = {}, {}
+    with jax.named_scope("tokens_run"):
+        for d in (1, 2, 3):
+            ts[d].wait_recv()
+        run = tok_in.at[shard, pl.ds(pl.multiple_of((b % 2) * 64, 64), 64)]
+        for d in (1, 2, 3):
+            tr[d] = send(run, run, tr_s.at[d - 1], tr_r.at[d - 1], r_dev[d])
+
+    with jax.named_scope("weight_grads_own_tokens"):
+
+        def step(t, _):
+            own[t] = dot(d_t[...], tok_cols(inner(t // 2, zh, t % 2)))
+            return 0
+
+        lax.fori_loop(0, 2 * NY, step, 0)
+
+    with jax.named_scope("tokens_x"):
+        for d in (1, 2, 3):
+            tr[d].wait_recv()
+        pair = tok_in.at[pl.ds(2 * x, 2)]
+        for d in (1, 3, 2):
+            tx[d] = send(pair, pair, tx_s.at[d - 1], tx_r.at[d - 1], x_dev[d])
 
     lane = lax.broadcasted_iota(jnp.int32, (TOK, 128), 1)
     low = lane < 64
+
+    def x_total(q, h):
+        cols = pl.ds(128 * h, 128)
+        total = x_out[x, q, :, cols].astype(F32)
+        for d in (1, 2, 3):
+            total = total + x_in[d - 1, q, :, cols].astype(F32)
+        return total
+
     with jax.named_scope("token_grads_run"):
-        for d in (1, 3, 2):
-            cx[d].wait_recv()
-
-        def x_total(q, h):
-            cols = pl.ds(128 * h, 128)
-            total = x_out[x, q, :, cols].astype(F32)
+        for m in range(2):
+            for d in (1, 3, 2):
+                cx[d, m].wait_recv()
+            for h in range(2):
+                even, odd = x_total(2 * m, h), x_total(2 * m + 1, h)
+                r_out[m, 2 * h] = jnp.where(low, even, pltpu.roll(odd, 64, 1)).astype(BF16)
+                r_out[m, 2 * h + 1] = jnp.where(low, pltpu.roll(even, 64, 1), odd).astype(BF16)
             for d in (1, 2, 3):
-                total = total + x_in[d - 1, q, :, cols].astype(F32)
-            return total
-
-        for h in range(2):
-            for m in range(2):
-                even, odd = x_total(2 * m, h), x_total(2 * m + 1, h)
-                r_out[2 * h, m] = jnp.where(low, even, pltpu.roll(odd, 64, 1)).astype(BF16)
-                r_out[2 * h + 1, m] = jnp.where(low, pltpu.roll(even, 64, 1), odd).astype(BF16)
-        for d in (1, 2, 3):
-            cr[d] = send(
-                r_out.at[(b + d) % NB], r_in.at[d - 1], cr_s.at[d - 1], cr_r.at[d - 1], r_dev[d]
+                cr[d, m] = send(
+                    r_out.at[m, (b + d) % NB], r_in.at[m, d - 1],
+                    cr_s.at[m, d - 1], cr_r.at[m, d - 1], r_dev[d],
+                )
+
+    bc, by = {}, {}
+    factor = 1.0 / math.sqrt(16 * TOK)
+
+    def whole(t, rows):
+        return own[t, rows, :] + dot(d_in[rows, :], tok_in[t])
+
+    def to_core(k):
+        at, n = CHUNKS[k]
+        rows = pl.ds(at, n)
+        bz[k].wait_recv()
+        for yy in range(NY):
+            c_out[yy, rows, :] = whole(2 * yy + 1 - c, rows).astype(BF16)
+        bc[k] = send(c_out.at[:, rows], c_in.at[:, rows], bc_s.at[k], bc_r.at[k], c_dev)
+
+    def to_y(k):
+        at, n = CHUNKS[k]
+        rows = pl.ds(at, n)
+        bc[k].wait_recv()
+        for d in (1, 3, 2, 0):
+            yy = (y + d) % NY
+            total = whole(2 * yy + c, rows) + c_in[yy, rows, :].astype(F32)
+            if d == 0:
+                wg_ref[rows, :] = total
+                continue
+            y_out[d - 1, rows, :] = total.astype(BF16)
+            by[d, k] = send(
+                y_out.at[d - 1, rows], y_in.at[d - 1, rows],
+                by_s.at[k, d - 1], by_r.at[k, d - 1], y_dev[d],
             )
 
-    with jax.named_scope("weight_grads_own"):
-        for d in (1, 3, 2):
-            by[d, 1, 0].wait_recv()
-        for at, n in CHUNKS:
-            rows = pl.ds(at, n)
-            total = own[1, rows, :]
+    def finish(k):
+        at, n = CHUNKS[k]
+        rows = pl.ds(at, n)
+        total = wg_ref[rows, :]
+        for d in (1, 3, 2):
+            by[d, k].wait_recv()
+            total = total + y_in[d - 1, rows, :].astype(F32)
+        wg_ref[rows, :] = total * factor
+
+    with jax.named_scope("weight_grads_first"):
+        for d in (1, 3, 2):
+            tx[d].wait_recv()
+        to_core(0)
+        to_core(1)
+        to_y(0)
+
+    with jax.named_scope("token_grads_strided"):
+        for m in range(2):
             for d in (1, 2, 3):
-                total = total + y_in[d - 1, 1, rows, :].astype(F32)
-            own[1, rows, :] = total
-
-    with jax.named_scope("token_grads_strided"):
-        for d in (1, 2, 3):
-            cr[d].wait_recv()
-        for m in range(2):
-            total = r_out[b, m].astype(F32)
+                cr[d, m].wait_recv()
+            total = r_out[m, b].astype(F32)
             for d in (1, 2, 3):
-                total = total + r_in[d - 1, m].astype(F32)
+                total = total + r_in[m, d - 1].astype(F32)
             turned = pltpu.roll(total, 64, 1)
             s_out[2 * m] = jnp.where(low[:64], total[:64], turned[64:]).astype(BF16)
             s_out[2 * m + 1] = jnp.where(low[:64], turned[:64], total[64:]).astype(BF16)
@@ -257,6 +287,17 @@
             cs[d] = send(
                 s_out.at[(a + d) % NA], s_in.at[d - 1], cs_s.at[d - 1], cs_r.at[d - 1], s_dev[d]
             )
+
+    with jax.named_scope("weight_grads_last"):
+        to_y(1)
+        for k in range(2, NCH):
+            to_core(k)
+            finish(k - 2)
+            to_y(k)
+        for k in range(NCH - 2, NCH):
+            finish(k)
+
+    with jax.named_scope("token_grads_last"):
         for d in (1, 2, 3):
             cs[d].wait_recv()
         total = s_out[a].astype(F32)
@@ -264,13 +305,6 @@
             total = total + s_in[d - 1].astype(F32)
         tg_ref[:64, :] = total[:, :64]
         tg_ref[64:, :] = pltpu.roll(total, 64, 1)[:, :64]
-
-    with jax.named_scope("weight_grads_last"):
-        factor = 1.0 / math.sqrt(16 * TOK)
-        for k, (at, n) in enumerate(CHUNKS):
-            rows = pl.ds(at, n)
-            bz[k].wait_recv()
-            wg_ref[rows, :] = (own[1, rows, :] + z_in[rows, :].astype(F32)) * factor
 
     for copy in sent:
         copy.wait_send()
@@ -302,25 +336,29 @@
             pltpu.VMEM((ROWS, TOK), BF16),
             pltpu.VMEM((384, TOK), F32),
             pltpu.VMEM((TOK, 384), BF16),
+            pltpu.VMEM((ROWS, TOK), BF16),
+            pltpu.VMEM((2 * NY, TOK, COLS), BF16),
             pltpu.VMEM((NX, 4, TOK, COLS), BF16),
             pltpu.VMEM((NX - 1, 4, TOK, COLS), BF16),
-            pltpu.VMEM((NB, 2, TOK, 128), BF16),
-            pltpu.VMEM((NB - 1, 2, TOK, 128), BF16),
+            pltpu.VMEM((2, NB, TOK, 128), BF16),
+            pltpu.VMEM((2, NB - 1, TOK, 128), BF16),
             pltpu.VMEM((NA, 64, 128), BF16),
             pltpu.VMEM((NA - 1, 64, 128), BF16),
-            pltpu.VMEM((8, ROWS, COLS), BF16),
-            pltpu.VMEM((8, ROWS, COLS), BF16),
-            pltpu.VMEM((2, ROWS, COLS), F32),
-            pltpu.VMEM((NY - 1, 2, ROWS, COLS), BF16),
-            pltpu.VMEM((NY - 1, 2, ROWS, COLS), BF16),
-            pltpu.VMEM((ROWS, COLS), BF16),
-            pltpu.VMEM((ROWS, COLS), BF16),
+            pltpu.VMEM((NY, ROWS, COLS), BF16),
+            pltpu.VMEM((NY, ROWS, COLS), BF16),
+            pltpu.VMEM((2 * NY, ROWS, COLS), F32),
+            pltpu.VMEM((NY - 1, ROWS, COLS), BF16),
+            pltpu.VMEM((NY - 1, ROWS, COLS), BF16),
             dma((NCH,)), dma((NCH,)),
             dma((NY, 1 + NCH)), dma((NY, 1 + NCH)),
             dma((NY, 1 + NCH)), dma((NY, 1 + NCH)),
-            dma((8,)), dma((8,)),
-            dma((NY - 1, 1 + NCH)), dma((NY - 1, 1 + NCH)),
             dma((NCH,)), dma((NCH,)),
+            dma((NCH,)), dma((NCH,)),
+            dma((NCH, 3)), dma((NCH, 3)),
+            dma((2, 3)), dma((2, 3)),
+            dma((2, 3)), dma((2, 3)),
+            dma((3,)), dma((3,)),
+            dma((1,)), dma((1,)),
             dma((3,)), dma((3,)),
             dma((3,)), dma((3,)),
             dma((3,)), dma((3,)),

time: 131 us -> 128 us (0.977)
  Pallas kernels: 126 us -> 123 us
    pallas_call x1, Pallas kernels: 126 us -> 123 us  [local(): pl.pallas_call(kernel, out_shape=(jax.ShapeDtypeStruct((HALF, TOK), BF16)...]
where the time goes in v2:
time: 128 us
  Pallas kernels  123 us (96%)
  local copies, waits for them, and re-layouts  3.36 us (3%)
    pallas_call x1, Pallas kernels, local(): pl.pallas_call(kernel, out_shape=(jax.ShapeDtypeStruct((HALF, TOK), BF16)...  123 us
    unnamed x11, local copies, waits for them, and re-layouts  2.6 us

profile of v2, /device:TPU:1, one launch (start us, length us, event | category | flops | bytes accessed | tf_op | source)
XLA Modules:
  0.0 127.6 jit_solution(15956710321446575387)
XLA Ops:
  0.6 0.0 copy-start
  0.6 0.0 copy-start.3
  0.7 0.0 copy-start.2
  0.7 0.0 copy-start.1
  0.7 0.6 copy-done
  1.3 0.1 copy-done.3
  1.4 0.1 copy.14
  1.6 0.0 copy-done.2
  1.6 0.2 fusion
  1.9 0.1 copy-done.1
  2.0 123.3 %ffn_grads.1 = (bf16[176,128]{1,0:T(8,128)(2,1)S(1)}, f32[128,64]{1,0:T(8,128)S(1)}, f32[352,256]{1,0:T(8,128)S(1)}) custom-call(bf16[352,256]{1,0:T(8,128)(2,1)S(1)} %bitcast.12, bf16[128,4096]{1,0:T(8,128)(2,1)S(1)} %copy-done.1, bf16[176,128]{1,0:T(8,128)(2,1)S(1)} %pad.9.gh_ref), custom_call_target="tpu_custom_call" | custom-call | tf_op jit(solution)/shard_map/ffn_grads/pallas_call | solution.py:324
  125.3 0.6 slice_bitcast_fusion
  125.9 0.7 copy.13
  126.6 1.0 copy.18
  (4 shorter events, 0.0 us)
Async XLA Ops:
  0.6 0.7 copy-start
  0.6 0.8 copy-start.3
  0.7 0.9 copy-start.2
  0.7 1.3 %copy-start.1 = (bf16[128,4096]{1,0:T(8,128)(2,1)S(1)}, bf16[128,4096]{1,0:T(8,128)(2,1)}, u32[]{:S(2)}) copy-start(bf16[128,4096]{1,0:T(8,128)(2,1)} %tok_ref.1) | copy-start | bytes 3145732

commit v3 on v2

--- a/solution.py
+++ b/solution.py
@@ -17,8 +17,10 @@
 ROWS = 2 * HALF
 COLS = 256
 TOK = 128
-CHUNKS = ((0, 96), (96, 96), (192, 96), (288, 64))
+CHUNKS = ((0, 80), (176, 80), (80, 64), (256, 64), (144, 32), (320, 32))
 NCH = len(CHUNKS)
+D_CHUNKS = ((0, 96), (96, 96), (192, 96), (288, 64))
+NDC = len(D_CHUNKS)
 
 
 def dot(a, b):
@@ -31,13 +33,13 @@
 
 def kernel(
     wt_ref, tok_ref, gh_ref, hid_ref, tg_ref, wg_ref,
-    w_all, acc, d_t, d_f, d_b, d_in, tok_in,
+    w_all, w_mid, tok_mid, acc, d_t, d_f, d_b, d_in, tok_in,
     x_out, x_in, r_out, r_in, s_out, s_in,
     c_out, c_in, own, y_out, y_in,
-    fz_s, fz_r, fy_s, fy_r, fc_s, fc_r,
+    near, f1_s, f1_r, fz_s, fz_r, fy_s, fy_r, fc_s, fc_r,
     bz_s, bz_r, bc_s, bc_r, by_s, by_r,
     cx_s, cx_r, cr_s, cr_r, cs_s, cs_r,
-    ta_s, ta_r, ts_s, ts_r, tr_s, tr_r, tx_s, tx_r,
+    tm_s, tm_r, ta_s, ta_r, ts_s, ts_r, tr_s, tr_r, tx_s, tx_r,
 ):
     me = lax.axis_index("inner")
     ou = lax.axis_index("outer")
@@ -48,7 +50,14 @@
     def inner(yy, zz, cc):
         return yy * 4 + zz * 2 + cc
 
+    z = zh * NZ + zl
+
+    def along(hops):
+        far = (z + hops) % (2 * NZ)
+        return {"inner": inner(y, far // NZ, c), "outer": x * NZ + far % NZ}
+
     z_dev = {"inner": inner(y, 1 - zh, c)}
+    leg = [along(8), along(24)]
     c_dev = {"inner": inner(y, zh, 1 - c)}
     y_dev = [{"inner": inner((y + d) % NY, zh, c)} for d in range(NY)]
     x_dev = [{"outer": ((x + d) % NX) * NZ + zl} for d in range(NX)]
@@ -67,50 +76,64 @@
         return copy
 
     barrier = pltpu.get_barrier_semaphore()
-    peers = [z_dev] + s_dev[1:] + x_dev[1:] + y_dev[1:] + r_dev[1:] + [c_dev]
+    quarter = [along(4), along(28)]
+    peers = leg + quarter + x_dev[1:] + y_dev[1:] + r_dev[1:] + [c_dev]
     for device in peers:
         pl.semaphore_signal(barrier, inc=1, device_id=device, device_id_type=MESH)
     w_all[me] = wt_ref[...]
     acc[...] = jnp.zeros_like(acc)
     pl.semaphore_wait(barrier, len(peers))
+    for device in quarter:
+        pl.semaphore_signal(near, inc=1, device_id=device, device_id_type=MESH)
 
     with jax.named_scope("gather_weights"):
-        fz, fy, fc = {}, {}, {}
-        shard_rows = pl.ds(pl.multiple_of((b % 2) * 64 + a * 16, 16), 16)
+        f1, fz, fy, fc = {}, {}, {}, {}
         shard = 2 * x + b // 2
+
+        def shard_rows(aa):
+            return pl.ds(pl.multiple_of((b % 2) * 64 + aa * 16, 16), 16)
+
+        mine = shard_rows(a)
         shard_cols = inner(shard // 2, 1 - zh, shard % 2)
         shard_cols = pl.ds(pl.multiple_of(shard_cols * COLS, COLS), COLS)
-        ta = send(
-            tok_ref.at[shard_rows, shard_cols], tok_in.at[shard, shard_rows],
-            ta_s.at[0], ta_r.at[0], z_dev,
+        tok_leg = along(8 + 16 * c)
+        tm = send(
+            tok_ref.at[mine, shard_cols], tok_mid, tm_s.at[0], tm_r.at[0], tok_leg
         )
         for k, (at, n) in enumerate(CHUNKS):
             part = w_all.at[me, pl.ds(at, n)]
-            fz[k] = send(part, part, fz_s.at[k], fz_r.at[k], z_dev)
-        mine = w_all.at[me]
+            f1[k] = send(part, w_mid.at[pl.ds(at, n)], f1_s.at[k], f1_r.at[k], leg[k % 2])
+        block = w_all.at[me]
         for d in (1, 3, 2):
-            fy[d, 0] = send(mine, mine, fy_s.at[d, 0], fy_r.at[d, 0], y_dev[d])
-        fc[0, 0] = send(mine, mine, fc_s.at[0, 0], fc_r.at[0, 0], c_dev)
+            fy[d, 0] = send(block, block, fy_s.at[d, 0], fy_r.at[d, 0], y_dev[d])
+        fc[0, 0] = send(block, block, fc_s.at[0, 0], fc_r.at[0, 0], c_dev)
+
+        def relay(k):
+            at, n = CHUNKS[k]
+            f1[k].wait_recv()
+            origin = (z + (24 if k % 2 == 0 else 8)) % (2 * NZ) // NZ
+            fz[k] = send(
+                w_mid.at[pl.ds(at, n)], w_all.at[inner(y, origin, c), pl.ds(at, n)],
+                fz_s.at[k], fz_r.at[k], leg[k % 2],
+            )
 
         def tok_cols(j):
             return tok_ref[:, pl.ds(pl.multiple_of(j * COLS, COLS), COLS)]
 
-        for d in (1, 3, 2):
-            fy[d, 0].wait_recv()
-            block = w_all.at[inner((y - d + NY) % NY, zh, c)]
-            fc[d, 0] = send(block, block, fc_s.at[d, 0], fc_r.at[d, 0], c_dev)
-        for d in range(NY):
-            fc[d, 0].wait_recv()
-
         def add_blocks(side, at, n):
-            def step(t, _):
+            total = acc[pl.ds(at, n), :]
+            for t in range(2 * NY):
                 j = inner(t // 2, side, t % 2)
-                acc[pl.ds(at, n), :] += dot_nt(w_all[j, pl.ds(at, n), :], tok_cols(j))
-                return 0
-
-            lax.fori_loop(0, 2 * NY, step, 0)
-
-        add_blocks(zh, 0, ROWS)
+                total = total + dot_nt(w_all[j, pl.ds(at, n), :], tok_cols(j))
+            acc[pl.ds(at, n), :] = total
+
+        def spread(k):
+            at, n = CHUNKS[k]
+            fz[k].wait_recv()
+            part = w_all.at[inner(y, 1 - zh, c), pl.ds(at, n)]
+            for d in (1, 3, 2):
+                fy[d, 1 + k] = send(part, part, fy_s.at[d, 1 + k], fy_r.at[d, 1 + k], y_dev[d])
+            fc[0, 1 + k] = send(part, part, fc_s.at[0, 1 + k], fc_r.at[0, 1 + k], c_dev)
 
         def pass_on(k):
             at, n = CHUNKS[k]
@@ -125,22 +148,48 @@
                 fc[d, 1 + k].wait_recv()
             add_blocks(1 - zh, at, n)
 
-        for k, (at, n) in enumerate(CHUNKS):
-            fz[k].wait_recv()
-            part = w_all.at[inner(y, 1 - zh, c), pl.ds(at, n)]
-            for d in (1, 3, 2):
-                fy[d, 1 + k] = send(part, part, fy_s.at[d, 1 + k], fy_r.at[d, 1 + k], y_dev[d])
-            fc[0, 1 + k] = send(part, part, fc_s.at[0, 1 + k], fc_r.at[0, 1 + k], c_dev)
-            if k > 0:
-                pass_on(k - 1)
-                use(k - 1)
+        tm.wait_recv()
+        ta = send(
+            tok_mid, tok_in.at[shard, shard_rows((a + 2) % NA)], ta_s.at[0], ta_r.at[0], tok_leg
+        )
+        relay(0)
+        relay(1)
+        for d in (1, 3, 2):
+            fy[d, 0].wait_recv()
+            block = w_all.at[inner((y - d + NY) % NY, zh, c)]
+            fc[d, 0] = send(block, block, fc_s.at[d, 0], fc_r.at[d, 0], c_dev)
+        relay(2)
+        relay(3)
+        for d in range(NY):
+            fc[d, 0].wait_recv()
+        for at in range(0, ROWS, HALF):
+            add_blocks(zh, at, HALF)
+        spread(0)
+        spread(1)
+        relay(4)
+        relay(5)
+        pass_on(0)
+        pass_on(1)
+        spread(2)
+        spread(3)
+        use(0)
+        use(1)
+        pass_on(2)
+        pass_on(3)
+        spread(4)
+        spread(5)
         ta.wait_recv()
+        pl.semaphore_wait(near, 2)
         ts = {}
         for d in (1, 2, 3):
-            part = tok_in.at[shard, shard_rows]
+            part = tok_in.at[shard, mine]
             ts[d] = send(part, part, ts_s.at[d - 1], ts_r.at[d - 1], s_dev[d])
-        pass_on(NCH - 1)
-        use(NCH - 1)
+        use(2)
+        use(3)
+        pass_on(4)
+        pass_on(5)
+        use(4)
+        use(5)
 
     with jax.named_scope("activations"):
         gate = acc[:HALF, :]
@@ -154,7 +203,7 @@
         d_t[:HALF, :] = d_gate
         d_t[HALF:, :] = d_up
         bz = {}
-        for k, (at, n) in enumerate(CHUNKS):
+        for k, (at, n) in enumerate(D_CHUNKS):
             rows = pl.ds(at, n)
             bz[k] = send(d_t.at[rows], d_in.at[rows], bz_s.at[k], bz_r.at[k], z_dev)
         d_f[:HALF, :] = d_gate.astype(F32)
@@ -168,11 +217,8 @@
             for d in (1, 3, 2, 0):
                 xb = (x + d) % NX
 
-                def step(q, _, xb=xb):
+                for q in range(2 * m, 2 * m + 2):
                     x_out[xb, q] = dot(d_b[:, :ROWS], w_all[4 * xb + q]).astype(BF16)
-                    return 0
-
-                lax.fori_loop(2 * m, 2 * m + 2, step, 0)
                 if d > 0:
                     pair = pl.ds(2 * m, 2)
                     cx[d, m] = send(
@@ -196,13 +242,6 @@
 
         lax.fori_loop(0, 2 * NY, step, 0)
 
-    with jax.named_scope("tokens_x"):
-        for d in (1, 2, 3):
-            tr[d].wait_recv()
-        pair = tok_in.at[pl.ds(2 * x, 2)]
-        for d in (1, 3, 2):
-            tx[d] = send(pair, pair, tx_s.at[d - 1], tx_r.at[d - 1], x_dev[d])
-
     lane = lax.broadcasted_iota(jnp.int32, (TOK, 128), 1)
     low = lane < 64
 
@@ -213,8 +252,8 @@
             total = total + x_in[d - 1, q, :, cols].astype(F32)
         return total
 
-    with jax.named_scope("token_grads_run"):
-        for m in range(2):
+    for m in range(2):
+        with jax.named_scope("token_grads_run"):
             for d in (1, 3, 2):
                 cx[d, m].wait_recv()
             for h in range(2):
@@ -226,6 +265,13 @@
                     r_out.at[m, (b + d) % NB], r_in.at[m, d - 1],
                     cr_s.at[m, d - 1], cr_r.at[m, d - 1], r_dev[d],
                 )
+        if m == 0:
+            with jax.named_scope("tokens_x"):
+                for d in (1, 2, 3):
+                    tr[d].wait_recv()
+                pair = tok_in.at[pl.ds(2 * x, 2)]
+                for d in (1, 3, 2):
+                    tx[d] = send(pair, pair, tx_s.at[d - 1], tx_r.at[d - 1], x_dev[d])
 
     bc, by = {}, {}
     factor = 1.0 / math.sqrt(16 * TOK)
@@ -234,7 +280,7 @@
         return own[t, rows, :] + dot(d_in[rows, :], tok_in[t])
 
     def to_core(k):
-        at, n = CHUNKS[k]
+        at, n = D_CHUNKS[k]
         rows = pl.ds(at, n)
         bz[k].wait_recv()
         for yy in range(NY):
@@ -242,7 +288,7 @@
         bc[k] = send(c_out.at[:, rows], c_in.at[:, rows], bc_s.at[k], bc_r.at[k], c_dev)
 
     def to_y(k):
-        at, n = CHUNKS[k]
+        at, n = D_CHUNKS[k]
         rows = pl.ds(at, n)
         bc[k].wait_recv()
         for d in (1, 3, 2, 0):
@@ -258,7 +304,7 @@
             )
 
     def finish(k):
-        at, n = CHUNKS[k]
+        at, n = D_CHUNKS[k]
         rows = pl.ds(at, n)
         total = wg_ref[rows, :]
         for d in (1, 3, 2):
@@ -270,8 +316,6 @@
         for d in (1, 3, 2):
             tx[d].wait_recv()
         to_core(0)
-        to_core(1)
-        to_y(0)
 
     with jax.named_scope("token_grads_strided"):
         for m in range(2):
@@ -289,12 +333,14 @@
             )
 
     with jax.named_scope("weight_grads_last"):
+        to_core(1)
+        to_y(0)
         to_y(1)
-        for k in range(2, NCH):
+        for k in range(2, NDC):
             to_core(k)
             finish(k - 2)
             to_y(k)
-        for k in range(NCH - 2, NCH):
+        for k in range(NDC - 2, NDC):
             finish(k)
 
     with jax.named_scope("token_grads_last"):
@@ -332,6 +378,8 @@
         out_specs=(vmem,) * 3,
         scratch_shapes=[
             pltpu.VMEM((16, ROWS, COLS), BF16),
+            pltpu.VMEM((ROWS, COLS), BF16),
+            pltpu.VMEM((16, COLS), BF16),
             pltpu.VMEM((ROWS, TOK), F32),
             pltpu.VMEM((ROWS, TOK), BF16),
             pltpu.VMEM((384, TOK), F32),
@@ -349,15 +397,18 @@
             pltpu.VMEM((2 * NY, ROWS, COLS), F32),
             pltpu.VMEM((NY - 1, ROWS, COLS), BF16),
             pltpu.VMEM((NY - 1, ROWS, COLS), BF16),
+            pltpu.SemaphoreType.REGULAR,
+            dma((NCH,)), dma((NCH,)),
             dma((NCH,)), dma((NCH,)),
             dma((NY, 1 + NCH)), dma((NY, 1 + NCH)),
             dma((NY, 1 + NCH)), dma((NY, 1 + NCH)),
-            dma((NCH,)), dma((NCH,)),
-            dma((NCH,)), dma((NCH,)),
-            dma((NCH, 3)), dma((NCH, 3)),
+            dma((NDC,)), dma((NDC,)),
+            dma((NDC,)), dma((NDC,)),
+            dma((NDC, 3)), dma((NDC, 3)),
             dma((2, 3)), dma((2, 3)),
             dma((2, 3)), dma((2, 3)),
             dma((3,)), dma((3,)),
+            dma((1,)), dma((1,)),
             dma((1,)), dma((1,)),
             dma((3,)), dma((3,)),
             dma((3,)), dma((3,)),

time: 128 us -> 122 us (0.953)
  Pallas kernels: 123 us -> 117 us
    pallas_call x1, Pallas kernels: 123 us -> 117 us  [local(): pl.pallas_call(kernel, out_shape=(jax.ShapeDtypeStruct((HALF, TOK), BF16)...]
where the time goes in v3:
time: 122 us; the launch traced here: 121 us
  Pallas kernels  117 us (96%)
  local copies, waits for them, and re-layouts  3.36 us (3%)
    pallas_call x1, Pallas kernels, local(): pl.pallas_call(kernel, out_shape=(jax.ShapeDtypeStruct((HALF, TOK), BF16)...  117 us
    unnamed x11, local copies, waits for them, and re-layouts  2.6 us

profile of v3, /device:TPU:1, one launch (start us, length us, event | category | flops | bytes accessed | tf_op | source)
XLA Modules:
  0.0 121.4 jit_solution(15265334849016098869)
XLA Ops:
  0.6 0.0 copy-start
  0.6 0.0 copy-start.3
  0.7 0.0 copy-start.2
  0.7 0.0 copy-start.1
  0.7 0.6 copy-done
  1.3 0.1 copy-done.3
  1.4 0.1 copy.14
  1.6 0.0 copy-done.2
  1.6 0.2 fusion
  1.9 0.1 copy-done.1
  2.0 117.0 %ffn_grads.1 = (bf16[176,128]{1,0:T(8,128)(2,1)S(1)}, f32[128,64]{1,0:T(8,128)S(1)}, f32[352,256]{1,0:T(8,128)S(1)}) custom-call(bf16[352,256]{1,0:T(8,128)(2,1)S(1)} %bitcast.12, bf16[128,4096]{1,0:T(8,128)(2,1)S(1)} %copy-done.1, bf16[176,128]{1,0:T(8,128)(2,1)S(1)} %pad.9.gh_ref), custom_call_target="tpu_custom_call" | custom-call | tf_op jit(solution)/shard_map/ffn_grads/pallas_call | solution.py:370
  119.1 0.6 slice_bitcast_fusion
  119.7 0.7 copy.13
  120.4 1.0 copy.18
  (4 shorter events, 0.0 us)
Async XLA Ops:
  0.6 0.7 copy-start
  0.6 0.8 copy-start.3
  0.7 0.9 copy-start.2
  0.7 1.3 %copy-start.1 = (bf16[128,4096]{1,0:T(8,128)(2,1)S(1)}, bf16[128,4096]{1,0:T(8,128)(2,1)}, u32[]{:S(2)}) copy-start(bf16[128,4096]{1,0:T(8,128)(2,1)} %tok_ref.1) | copy-start | bytes 3145732

commit v4 on v3

--- a/solution.py
+++ b/solution.py
@@ -19,8 +19,6 @@
 TOK = 128
 CHUNKS = ((0, 80), (176, 80), (80, 64), (256, 64), (144, 32), (320, 32))
 NCH = len(CHUNKS)
-D_CHUNKS = ((0, 96), (96, 96), (192, 96), (288, 64))
-NDC = len(D_CHUNKS)
 
 
 def dot(a, b):
@@ -34,11 +32,11 @@
 def kernel(
     wt_ref, tok_ref, gh_ref, hid_ref, tg_ref, wg_ref,
     w_all, w_mid, tok_mid, acc, d_t, d_f, d_b, d_in, tok_in,
-    x_out, x_in, r_out, r_in, s_out, s_in,
+    x_out, x_mid, x_in, r_out, r_in, s_out, s_in,
     c_out, c_in, own, y_out, y_in,
     near, f1_s, f1_r, fz_s, fz_r, fy_s, fy_r, fc_s, fc_r,
     bz_s, bz_r, bc_s, bc_r, by_s, by_r,
-    cx_s, cx_r, cr_s, cr_r, cs_s, cs_r,
+    cm_s, cm_r, cx_s, cx_r, cr_s, cr_r, cs_s, cs_r,
     tm_s, tm_r, ta_s, ta_r, ts_s, ts_r, tr_s, tr_r, tx_s, tx_r,
 ):
     me = lax.axis_index("inner")
@@ -172,67 +170,101 @@
         pass_on(1)
         spread(2)
         spread(3)
+        ta.wait_recv()
+        pl.semaphore_wait(near, 2)
+        ts = {}
+        for d in (1, 2, 3):
+            part = tok_in.at[shard, mine]
+            ts[d] = send(part, part, ts_s.at[d - 1], ts_r.at[d - 1], s_dev[d])
+
+    bz = {}
+
+    def activate(p):
+        at, n = CHUNKS[2 * p]
+        gate_rows, up_rows = pl.ds(at, n), pl.ds(HALF + at, n)
+        gate = acc[gate_rows, :]
+        up = acc[up_rows, :]
+        sig = jax.nn.sigmoid(gate)
+        silu = gate * sig
+        hid_ref[gate_rows, :] = (silu * up).astype(BF16)
+        cot = gh_ref[gate_rows, :].astype(F32)
+        d_gate = (cot * up * sig * (1.0 + gate * (1.0 - sig))).astype(BF16)
+        d_up = (cot * silu).astype(BF16)
+        d_t[gate_rows, :] = d_gate
+        d_t[up_rows, :] = d_up
+        d_f[gate_rows, :] = d_gate.astype(F32)
+        d_f[up_rows, :] = d_up.astype(F32)
+
+    def send_d(p):
+        for k in (2 * p, 2 * p + 1):
+            rows = pl.ds(*CHUNKS[k])
+            bz[k] = send(d_t.at[rows], d_in.at[rows], bz_s.at[k], bz_r.at[k], z_dev)
+
+    with jax.named_scope("activations"):
         use(0)
         use(1)
         pass_on(2)
         pass_on(3)
+        activate(0)
         spread(4)
         spread(5)
-        ta.wait_recv()
-        pl.semaphore_wait(near, 2)
-        ts = {}
-        for d in (1, 2, 3):
-            part = tok_in.at[shard, mine]
-            ts[d] = send(part, part, ts_s.at[d - 1], ts_r.at[d - 1], s_dev[d])
+        send_d(0)
         use(2)
         use(3)
+        activate(1)
+        send_d(1)
         pass_on(4)
         pass_on(5)
         use(4)
         use(5)
-
-    with jax.named_scope("activations"):
-        gate = acc[:HALF, :]
-        up = acc[HALF:, :]
-        sig = jax.nn.sigmoid(gate)
-        silu = gate * sig
-        hid_ref[...] = (silu * up).astype(BF16)
-        cot = gh_ref[...].astype(F32)
-        d_gate = (cot * up * sig * (1.0 + gate * (1.0 - sig))).astype(BF16)
-        d_up = (cot * silu).astype(BF16)
-        d_t[:HALF, :] = d_gate
-        d_t[HALF:, :] = d_up
-        bz = {}
-        for k, (at, n) in enumerate(D_CHUNKS):
-            rows = pl.ds(at, n)
-            bz[k] = send(d_t.at[rows], d_in.at[rows], bz_s.at[k], bz_r.at[k], z_dev)
-        d_f[:HALF, :] = d_gate.astype(F32)
-        d_f[HALF:ROWS, :] = d_up.astype(F32)
+        activate(2)
+        send_d(2)
         d_f[ROWS:, :] = jnp.zeros((d_f.shape[0] - ROWS, TOK), F32)
         d_b[...] = d_f[...].T.astype(BF16)
 
-    cx, cr, cs = {}, {}, {}
+    cm, cx, cr, cs = {}, {}, {}, {}
+    tr, tx = {}, {}
+
+    def term(xb, q):
+        return dot(d_b[:, :ROWS], w_all[4 * xb + q])
+
+    def send_x(step, q):
+        side = 0 if step == 1 else 1
+        cx[side, q] = send(
+            x_out.at[(x + step) % NX, q], x_in.at[side, q],
+            cx_s.at[side, q], cx_r.at[side, q], x_dev[step],
+        )
+
     with jax.named_scope("token_grads_x"):
-        for m in range(2):
-            for d in (1, 3, 2, 0):
-                xb = (x + d) % NX
-
-                for q in range(2 * m, 2 * m + 2):
-                    x_out[xb, q] = dot(d_b[:, :ROWS], w_all[4 * xb + q]).astype(BF16)
-                if d > 0:
-                    pair = pl.ds(2 * m, 2)
-                    cx[d, m] = send(
-                        x_out.at[xb, pair], x_in.at[d - 1, pair],
-                        cx_s.at[m, d - 1], cx_r.at[m, d - 1], x_dev[d],
-                    )
-
-    tr, tx = {}, {}
+        for q in range(4):
+            xb = (x + 2) % NX
+            x_out[xb, q] = term(xb, q).astype(BF16)
+            cm[q] = send(
+                x_out.at[xb, q], x_mid.at[q], cm_s.at[q], cm_r.at[q], x_dev[1 if q % 2 == 0 else 3]
+            )
+        for q in range(4):
+            step = 3 if q % 2 == 0 else 1
+            xb = (x + step) % NX
+            x_out[xb, q] = term(xb, q).astype(BF16)
+            send_x(step, q)
+
     with jax.named_scope("tokens_run"):
         for d in (1, 2, 3):
             ts[d].wait_recv()
         run = tok_in.at[shard, pl.ds(pl.multiple_of((b % 2) * 64, 64), 64)]
         for d in (1, 2, 3):
             tr[d] = send(run, run, tr_s.at[d - 1], tr_r.at[d - 1], r_dev[d])
+
+    with jax.named_scope("token_grads_x_sums"):
+        for q in range(4):
+            step = 1 if q % 2 == 0 else 3
+            xb = (x + step) % NX
+            part = term(xb, q)
+            cm[q].wait_recv()
+            x_out[xb, q] = (part + x_mid[q].astype(F32)).astype(BF16)
+            send_x(step, q)
+        for q in range(4):
+            x_out[x, q] = term(x, q).astype(BF16)
 
     with jax.named_scope("weight_grads_own_tokens"):
 
@@ -248,14 +280,15 @@
     def x_total(q, h):
         cols = pl.ds(128 * h, 128)
         total = x_out[x, q, :, cols].astype(F32)
-        for d in (1, 2, 3):
-            total = total + x_in[d - 1, q, :, cols].astype(F32)
+        for side in range(2):
+            total = total + x_in[side, q, :, cols].astype(F32)
         return total
 
     for m in range(2):
         with jax.named_scope("token_grads_run"):
-            for d in (1, 3, 2):
-                cx[d, m].wait_recv()
+            for q in range(2 * m, 2 * m + 2):
+                for side in range(2):
+                    cx[side, q].wait_recv()
             for h in range(2):
                 even, odd = x_total(2 * m, h), x_total(2 * m + 1, h)
                 r_out[m, 2 * h] = jnp.where(low, even, pltpu.roll(odd, 64, 1)).astype(BF16)
@@ -280,16 +313,15 @@
         return own[t, rows, :] + dot(d_in[rows, :], tok_in[t])
 
     def to_core(k):
-        at, n = D_CHUNKS[k]
-        rows = pl.ds(at, n)
-        bz[k].wait_recv()
+        rows = pl.ds(k * HALF, HALF)
+        for p in range(k, NCH, 2):
+            bz[p].wait_recv()
         for yy in range(NY):
             c_out[yy, rows, :] = whole(2 * yy + 1 - c, rows).astype(BF16)
         bc[k] = send(c_out.at[:, rows], c_in.at[:, rows], bc_s.at[k], bc_r.at[k], c_dev)
 
     def to_y(k):
-        at, n = D_CHUNKS[k]
-        rows = pl.ds(at, n)
+        rows = pl.ds(k * HALF, HALF)
         bc[k].wait_recv()
         for d in (1, 3, 2, 0):
             yy = (y + d) % NY
@@ -304,8 +336,7 @@
             )
 
     def finish(k):
-        at, n = D_CHUNKS[k]
-        rows = pl.ds(at, n)
+        rows = pl.ds(k * HALF, HALF)
         total = wg_ref[rows, :]
         for d in (1, 3, 2):
             by[d, k].wait_recv()
@@ -316,6 +347,7 @@
         for d in (1, 3, 2):
             tx[d].wait_recv()
         to_core(0)
+        to_core(1)
 
     with jax.named_scope("token_grads_strided"):
         for m in range(2):
@@ -333,15 +365,10 @@
             )
 
     with jax.named_scope("weight_grads_last"):
-        to_core(1)
         to_y(0)
         to_y(1)
-        for k in range(2, NDC):
-            to_core(k)
-            finish(k - 2)
-            to_y(k)
-        for k in range(NDC - 2, NDC):
-            finish(k)
+        finish(0)
+        finish(1)
 
     with jax.named_scope("token_grads_last"):
         for d in (1, 2, 3):
@@ -387,7 +414,8 @@
             pltpu.VMEM((ROWS, TOK), BF16),
             pltpu.VMEM((2 * NY, TOK, COLS), BF16),
             pltpu.VMEM((NX, 4, TOK, COLS), BF16),
-            pltpu.VMEM((NX - 1, 4, TOK, COLS), BF16),
+            pltpu.VMEM((4, TOK, COLS), BF16),
+            pltpu.VMEM((2, 4, TOK, COLS), BF16),
             pltpu.VMEM((2, NB, TOK, 128), BF16),
             pltpu.VMEM((2, NB - 1, TOK, 128), BF16),
             pltpu.VMEM((NA, 64, 128), BF16),
@@ -402,10 +430,11 @@
             dma((NCH,)), dma((NCH,)),
             dma((NY, 1 + NCH)), dma((NY, 1 + NCH)),
             dma((NY, 1 + NCH)), dma((NY, 1 + NCH)),
-            dma((NDC,)), dma((NDC,)),
-            dma((NDC,)), dma((NDC,)),
-            dma((NDC, 3)), dma((NDC, 3)),
+            dma((NCH,)), dma((NCH,)),
+            dma((2,)), dma((2,)),
             dma((2, 3)), dma((2, 3)),
+            dma((4,)), dma((4,)),
+            dma((2, 4)), dma((2, 4)),
             dma((2, 3)), dma((2, 3)),
             dma((3,)), dma((3,)),
             dma((1,)), dma((1,)),

time: 122 us -> 114 us (0.934)
  the two profiles are of different devices: /device:TPU:1 before, /device:TPU:97 now
where the time goes in v4:
time: 114 us; the launch traced here: 113 us
  Pallas kernels  109 us (96%)
  local copies, waits for them, and re-layouts  3.36 us (3%)
    pallas_call x1, Pallas kernels, local(): pl.pallas_call(kernel, out_shape=(jax.ShapeDtypeStruct((HALF, TOK), BF16)...  109 us
    unnamed x11, local copies, waits for them, and re-layouts  2.6 us

profile of v4, /device:TPU:97, one launch (start us, length us, event | category | flops | bytes accessed | tf_op | source)
XLA Modules:
  0.0 113.4 jit_solution(4207502633345648873)
XLA Ops:
  0.6 0.0 copy-start
  0.6 0.0 copy-start.3
  0.7 0.0 copy-start.2
  0.7 0.0 copy-start.1
  0.7 0.6 copy-done
  1.3 0.1 copy-done.3
  1.4 0.1 copy.14
  1.6 0.0 copy-done.2
  1.6 0.2 fusion
  1.9 0.1 copy-done.1
  2.0 109.1 %ffn_grads.1 = (bf16[176,128]{1,0:T(8,128)(2,1)S(1)}, f32[128,64]{1,0:T(8,128)S(1)}, f32[352,256]{1,0:T(8,128)S(1)}) custom-call(bf16[352,256]{1,0:T(8,128)(2,1)S(1)} %bitcast.12, bf16[128,4096]{1,0:T(8,128)(2,1)S(1)} %copy-done.1, bf16[176,128]{1,0:T(8,128)(2,1)S(1)} %pad.9.gh_ref), custom_call_target="tpu_custom_call" | custom-call | tf_op jit(solution)/shard_map/ffn_grads/pallas_call | solution.py:397
  111.1 0.6 slice_bitcast_fusion
  111.7 0.7 copy.13
  112.4 1.0 copy.18
  (4 shorter events, 0.0 us)
Async XLA Ops:
  0.6 0.7 copy-start
  0.6 0.8 copy-start.3
  0.7 0.9 copy-start.2
  0.7 1.3 %copy-start.1 = (bf16[128,4096]{1,0:T(8,128)(2,1)S(1)}, bf16[128,4096]{1,0:T(8,128)(2,1)}, u32[]{:S(2)}) copy-start(bf16[128,4096]{1,0:T(8,128)(2,1)} %tok_ref.1) | copy-start | bytes 3145732

commit v5 on v4

--- a/solution.py
+++ b/solution.py
@@ -32,7 +32,7 @@
 def kernel(
     wt_ref, tok_ref, gh_ref, hid_ref, tg_ref, wg_ref,
     w_all, w_mid, tok_mid, acc, d_t, d_f, d_b, d_in, tok_in,
-    x_out, x_mid, x_in, r_out, r_in, s_out, s_in,
+    x_out, x_mid, x_in, r_out, r_in, s_own, s_out, s_in,
     c_out, c_in, own, y_out, y_in,
     near, f1_s, f1_r, fz_s, fz_r, fy_s, fy_r, fc_s, fc_r,
     bz_s, bz_r, bc_s, bc_r, by_s, by_r,
@@ -219,92 +219,103 @@
         use(5)
         activate(2)
         send_d(2)
+        tr, tx = {}, {}
+        for d in (1, 2, 3):
+            ts[d].wait_recv()
+        run = tok_in.at[shard, pl.ds(pl.multiple_of((b % 2) * 64, 64), 64)]
+        for d in (1, 2, 3):
+            tr[d] = send(run, run, tr_s.at[d - 1], tr_r.at[d - 1], r_dev[d])
         d_f[ROWS:, :] = jnp.zeros((d_f.shape[0] - ROWS, TOK), F32)
         d_b[...] = d_f[...].T.astype(BF16)
 
     cm, cx, cr, cs = {}, {}, {}, {}
-    tr, tx = {}, {}
-
-    def term(xb, q):
-        return dot(d_b[:, :ROWS], w_all[4 * xb + q])
-
-    def send_x(step, q):
+    order = (1, 2, 3, 0)
+    quarters = [(a + i) % NA for i in range(NA)]
+
+    def term(xb, i):
+        return dot(d_b[:, :ROWS], w_all[4 * xb + quarters[i]])
+
+    def send_x(step, i):
         side = 0 if step == 1 else 1
-        cx[side, q] = send(
-            x_out.at[(x + step) % NX, q], x_in.at[side, q],
-            cx_s.at[side, q], cx_r.at[side, q], x_dev[step],
+        cx[side, i] = send(
+            x_out.at[(x + step) % NX, i], x_in.at[side, i],
+            cx_s.at[side, i], cx_r.at[side, i], x_dev[step],
         )
 
     with jax.named_scope("token_grads_x"):
-        for q in range(4):
+        for i in order:
             xb = (x + 2) % NX
-            x_out[xb, q] = term(xb, q).astype(BF16)
-            cm[q] = send(
-                x_out.at[xb, q], x_mid.at[q], cm_s.at[q], cm_r.at[q], x_dev[1 if q % 2 == 0 else 3]
+            x_out[xb, i] = term(xb, i).astype(BF16)
+            cm[i] = send(
+                x_out.at[xb, i], x_mid.at[i], cm_s.at[i], cm_r.at[i], x_dev[1 if i % 2 == 0 else 3]
             )
-        for q in range(4):
-            step = 3 if q % 2 == 0 else 1
+        for i in order:
+            step = 3 if i % 2 == 0 else 1
             xb = (x + step) % NX
-            x_out[xb, q] = term(xb, q).astype(BF16)
-            send_x(step, q)
-
-    with jax.named_scope("tokens_run"):
-        for d in (1, 2, 3):
-            ts[d].wait_recv()
-        run = tok_in.at[shard, pl.ds(pl.multiple_of((b % 2) * 64, 64), 64)]
-        for d in (1, 2, 3):
-            tr[d] = send(run, run, tr_s.at[d - 1], tr_r.at[d - 1], r_dev[d])
-
-    with jax.named_scope("token_grads_x_sums"):
-        for q in range(4):
-            step = 1 if q % 2 == 0 else 3
+            x_out[xb, i] = term(xb, i).astype(BF16)
+            send_x(step, i)
+        for i in order:
+            step = 1 if i % 2 == 0 else 3
             xb = (x + step) % NX
-            part = term(xb, q)
-            cm[q].wait_recv()
-            x_out[xb, q] = (part + x_mid[q].astype(F32)).astype(BF16)
-            send_x(step, q)
-        for q in range(4):
-            x_out[x, q] = term(x, q).astype(BF16)
-
-    with jax.named_scope("weight_grads_own_tokens"):
-
+            part = term(xb, i)
+            cm[i].wait_recv()
+            x_out[xb, i] = (part + x_mid[i].astype(F32)).astype(BF16)
+            send_x(step, i)
+        for i in order:
+            x_out[x, i] = term(x, i).astype(BF16)
+
+    low = lax.broadcasted_iota(jnp.int32, (64, 128), 1) < 64
+
+    def to_run(i):
+        for side in range(2):
+            cx[side, i].wait_recv()
+        for h in range(2):
+            cols = pl.ds(128 * h, 128)
+            total = x_out[x, i, :, cols].astype(F32)
+            for side in range(2):
+                total = total + x_in[side, i, :, cols].astype(F32)
+            turned = pltpu.roll(total, 64, 1)
+            r_out[i, 2 * h] = jnp.where(low, total[:64], turned[64:]).astype(BF16)
+            r_out[i, 2 * h + 1] = jnp.where(low, turned[:64], total[64:]).astype(BF16)
+        for d in (1, 2, 3):
+            cr[d, i] = send(
+                r_out.at[i, (b + d) % NB], r_in.at[i, d - 1],
+                cr_s.at[i, d - 1], cr_r.at[i, d - 1], r_dev[d],
+            )
+
+    def run_total(i):
+        for d in (1, 2, 3):
+            cr[d, i].wait_recv()
+        total = r_out[i, b].astype(F32)
+        for d in (1, 2, 3):
+            total = total + r_in[i, d - 1].astype(F32)
+        return total
+
+    def to_strided(i):
+        s_out[i - 1] = run_total(i).astype(BF16)
+        cs[i] = send(s_out.at[i - 1], s_in.at[i - 1], cs_s.at[i - 1], cs_r.at[i - 1], s_dev[i])
+
+    def own_tokens(first, last):
         def step(t, _):
             own[t] = dot(d_t[...], tok_cols(inner(t // 2, zh, t % 2)))
             return 0
 
-        lax.fori_loop(0, 2 * NY, step, 0)
-
-    lane = lax.broadcasted_iota(jnp.int32, (TOK, 128), 1)
-    low = lane < 64
-
-    def x_total(q, h):
-        cols = pl.ds(128 * h, 128)
-        total = x_out[x, q, :, cols].astype(F32)
-        for side in range(2):
-            total = total + x_in[side, q, :, cols].astype(F32)
-        return total
-
-    for m in range(2):
-        with jax.named_scope("token_grads_run"):
-            for q in range(2 * m, 2 * m + 2):
-                for side in range(2):
-                    cx[side, q].wait_recv()
-            for h in range(2):
-                even, odd = x_total(2 * m, h), x_total(2 * m + 1, h)
-                r_out[m, 2 * h] = jnp.where(low, even, pltpu.roll(odd, 64, 1)).astype(BF16)
-                r_out[m, 2 * h + 1] = jnp.where(low, pltpu.roll(even, 64, 1), odd).astype(BF16)
-            for d in (1, 2, 3):
-                cr[d, m] = send(
-                    r_out.at[m, (b + d) % NB], r_in.at[m, d - 1],
-                    cr_s.at[m, d - 1], cr_r.at[m, d - 1], r_dev[d],
-                )
-        if m == 0:
-            with jax.named_scope("tokens_x"):
-                for d in (1, 2, 3):
-                    tr[d].wait_recv()
-                pair = tok_in.at[pl.ds(2 * x, 2)]
-                for d in (1, 3, 2):
-                    tx[d] = send(pair, pair, tx_s.at[d - 1], tx_r.at[d - 1], x_dev[d])
+        lax.fori_loop(first, last, step, 0)
+
+    with jax.named_scope("token_grads_run"):
+        to_run(1)
+        own_tokens(0, 4)
+        to_run(2)
+        for d in (1, 2, 3):
+            tr[d].wait_recv()
+        pair = tok_in.at[pl.ds(2 * x, 2)]
+        for d in (1, 3, 2):
+            tx[d] = send(pair, pair, tx_s.at[d - 1], tx_r.at[d - 1], x_dev[d])
+        to_run(3)
+        own_tokens(4, 8)
+        to_run(0)
+        for i in (1, 2, 3):
+            to_strided(i)
 
     bc, by = {}, {}
     factor = 1.0 / math.sqrt(16 * TOK)
@@ -348,21 +359,7 @@
             tx[d].wait_recv()
         to_core(0)
         to_core(1)
-
-    with jax.named_scope("token_grads_strided"):
-        for m in range(2):
-            for d in (1, 2, 3):
-                cr[d, m].wait_recv()
-            total = r_out[m, b].astype(F32)
-            for d in (1, 2, 3):
-                total = total + r_in[m, d - 1].astype(F32)
-            turned = pltpu.roll(total, 64, 1)
-            s_out[2 * m] = jnp.where(low[:64], total[:64], turned[64:]).astype(BF16)
-            s_out[2 * m + 1] = jnp.where(low[:64], turned[:64], total[64:]).astype(BF16)
-        for d in (1, 2, 3):
-            cs[d] = send(
-                s_out.at[(a + d) % NA], s_in.at[d - 1], cs_s.at[d - 1], cs_r.at[d - 1], s_dev[d]
-            )
+        s_own[...] = run_total(0)
 
     with jax.named_scope("weight_grads_last"):
         to_y(0)
@@ -373,9 +370,9 @@
     with jax.named_scope("token_grads_last"):
         for d in (1, 2, 3):
             cs[d].wait_recv()
-        total = s_out[a].astype(F32)
-        for d in (1, 2, 3):
-            total = total + s_in[d - 1].astype(F32)
+        total = s_own[...]
+        for i in (1, 2, 3):
+            total = total + s_in[i - 1].astype(F32)
         tg_ref[:64, :] = total[:, :64]
         tg_ref[64:, :] = pltpu.roll(total, 64, 1)[:, :64]
 
@@ -416,9 +413,10 @@
             pltpu.VMEM((NX, 4, TOK, COLS), BF16),
             pltpu.VMEM((4, TOK, COLS), BF16),
             pltpu.VMEM((2, 4, TOK, COLS), BF16),
-            pltpu.VMEM((2, NB, TOK, 128), BF16),
-            pltpu.VMEM((2, NB - 1, TOK, 128), BF16),
-            pltpu.VMEM((NA, 64, 128), BF16),
+            pltpu.VMEM((NA, NB, 64, 128), BF16),
+            pltpu.VMEM((NA, NB - 1, 64, 128), BF16),
+            pltpu.VMEM((64, 128), F32),
+            pltpu.VMEM((NA - 1, 64, 128), BF16),
             pltpu.VMEM((NA - 1, 64, 128), BF16),
             pltpu.VMEM((NY, ROWS, COLS), BF16),
             pltpu.VMEM((NY, ROWS, COLS), BF16),
@@ -435,7 +433,7 @@
             dma((2, 3)), dma((2, 3)),
             dma((4,)), dma((4,)),
             dma((2, 4)), dma((2, 4)),
-            dma((2, 3)), dma((2, 3)),
+            dma((4, 3)), dma((4, 3)),
             dma((3,)), dma((3,)),
             dma((1,)), dma((1,)),
             dma((1,)), dma((1,)),

time: 114 us -> 113 us (level)
  the two profiles are of different devices: /device:TPU:97 before, /device:TPU:1 now
where the time goes in v5:
time: 113 us; the launch traced here: 112 us
  Pallas kernels  107 us (95%)
  local copies, waits for them, and re-layouts  3.36 us (3%)
    pallas_call x1, Pallas kernels, local(): pl.pallas_call(kernel, out_shape=(jax.ShapeDtypeStruct((HALF, TOK), BF16)...  107 us
    unnamed x11, local copies, waits for them, and re-layouts  2.6 us

profile of v5, /device:TPU:1, one launch (start us, length us, event | category | flops | bytes accessed | tf_op | source)
XLA Modules:
  0.0 111.5 jit_solution(14428718736067561832)
XLA Ops:
  0.6 0.0 copy-start
  0.6 0.0 copy-start.3
  0.7 0.0 copy-start.2
  0.7 0.0 copy-start.1
  0.7 0.6 copy-done
  1.3 0.1 copy-done.3
  1.4 0.1 copy.14
  1.6 0.0 copy-done.2
  1.6 0.2 fusion
  1.9 0.1 copy-done.1
  2.0 107.2 %ffn_grads.1 = (bf16[176,128]{1,0:T(8,128)(2,1)S(1)}, f32[128,64]{1,0:T(8,128)S(1)}, f32[352,256]{1,0:T(8,128)S(1)}) custom-call(bf16[352,256]{1,0:T(8,128)(2,1)S(1)} %bitcast.12, bf16[128,4096]{1,0:T(8,128)(2,1)S(1)} %copy-done.1, bf16[176,128]{1,0:T(8,128)(2,1)S(1)} %pad.9.gh_ref), custom_call_target="tpu_custom_call" | custom-call | tf_op jit(solution)/shard_map/ffn_grads/pallas_call | solution.py:394
  109.2 0.6 slice_bitcast_fusion
  109.8 0.7 copy.13
  110.5 1.0 copy.18
  (4 shorter events, 0.0 us)
Async XLA Ops:
  0.6 0.7 copy-start
  0.6 0.8 copy-start.3
  0.7 0.9 copy-start.2
  0.7 1.3 %copy-start.1 = (bf16[128,4096]{1,0:T(8,128)(2,1)S(1)}, bf16[128,4096]{1,0:T(8,128)(2,1)}, u32[]{:S(2)}) copy-start(bf16[128,4096]{1,0:T(8,128)(2,1)} %tok_ref.1) | copy-start | bytes 3145732

commit v6 on v5

--- a/solution.py
+++ b/solution.py
@@ -33,9 +33,9 @@
     wt_ref, tok_ref, gh_ref, hid_ref, tg_ref, wg_ref,
     w_all, w_mid, tok_mid, acc, d_t, d_f, d_b, d_in, tok_in,
     x_out, x_mid, x_in, r_out, r_in, s_own, s_out, s_in,
-    c_out, c_in, own, y_out, y_in,
+    tok_peer, d_peer, tok_in_peer, d_in_peer, own, y_out, y_in,
     near, f1_s, f1_r, fz_s, fz_r, fy_s, fy_r, fc_s, fc_r,
-    bz_s, bz_r, bc_s, bc_r, by_s, by_r,
+    bz_s, bz_r, bt_s, bt_r, bd_s, bd_r, bu_s, bu_r, be_s, be_r, by_s, by_r,
     cm_s, cm_r, cx_s, cx_r, cr_s, cr_r, cs_s, cs_r,
     tm_s, tm_r, ta_s, ta_r, ts_s, ts_r, tr_s, tr_r, tx_s, tx_r,
 ):
@@ -146,6 +146,12 @@
                 fc[d, 1 + k].wait_recv()
             add_blocks(1 - zh, at, n)
 
+        bt = {}
+        for yy in range(NY):
+            bt[yy] = send(
+                tok_ref.at[:, pl.ds(pl.multiple_of(inner(yy, zh, 1 - c) * COLS, COLS), COLS)],
+                tok_peer.at[yy], bt_s.at[yy], bt_r.at[yy], c_dev,
+            )
         tm.wait_recv()
         ta = send(
             tok_mid, tok_in.at[shard, shard_rows((a + 2) % NA)], ta_s.at[0], ta_r.at[0], tok_leg
@@ -158,6 +164,12 @@
             fc[d, 0] = send(block, block, fc_s.at[d, 0], fc_r.at[d, 0], c_dev)
         relay(2)
         relay(3)
+        ta.wait_recv()
+        pl.semaphore_wait(near, 2)
+        ts = {}
+        for d in (1, 2, 3):
+            part = tok_in.at[shard, mine]
+            ts[d] = send(part, part, ts_s.at[d - 1], ts_r.at[d - 1], s_dev[d])
         for d in range(NY):
             fc[d, 0].wait_recv()
         for at in range(0, ROWS, HALF):
@@ -170,14 +182,14 @@
         pass_on(1)
         spread(2)
         spread(3)
-        ta.wait_recv()
-        pl.semaphore_wait(near, 2)
-        ts = {}
-        for d in (1, 2, 3):
-            part = tok_in.at[shard, mine]
-            ts[d] = send(part, part, ts_s.at[d - 1], ts_r.at[d - 1], s_dev[d])
-
-    bz = {}
+        tr, tx = {}, {}
+        for d in (1, 2, 3):
+            ts[d].wait_recv()
+        run = tok_in.at[shard, pl.ds(pl.multiple_of((b % 2) * 64, 64), 64)]
+        for d in (1, 2, 3):
+            tr[d] = send(run, run, tr_s.at[d - 1], tr_r.at[d - 1], r_dev[d])
+
+    bz, bd = {}, {}
 
     def activate(p):
         at, n = CHUNKS[2 * p]
@@ -199,6 +211,7 @@
         for k in (2 * p, 2 * p + 1):
             rows = pl.ds(*CHUNKS[k])
             bz[k] = send(d_t.at[rows], d_in.at[rows], bz_s.at[k], bz_r.at[k], z_dev)
+            bd[k] = send(d_t.at[rows], d_peer.at[rows], bd_s.at[k], bd_r.at[k], c_dev)
 
     with jax.named_scope("activations"):
         use(0)
@@ -211,20 +224,19 @@
         send_d(0)
         use(2)
         use(3)
+        pass_on(4)
+        pass_on(5)
         activate(1)
         send_d(1)
-        pass_on(4)
-        pass_on(5)
+        for d in (1, 2, 3):
+            tr[d].wait_recv()
+        pair = tok_in.at[pl.ds(2 * x, 2)]
+        for d in (1, 3, 2):
+            tx[d] = send(pair, pair, tx_s.at[d - 1], tx_r.at[d - 1], x_dev[d])
         use(4)
         use(5)
         activate(2)
         send_d(2)
-        tr, tx = {}, {}
-        for d in (1, 2, 3):
-            ts[d].wait_recv()
-        run = tok_in.at[shard, pl.ds(pl.multiple_of((b % 2) * 64, 64), 64)]
-        for d in (1, 2, 3):
-            tr[d] = send(run, run, tr_s.at[d - 1], tr_r.at[d - 1], r_dev[d])
         d_f[ROWS:, :] = jnp.zeros((d_f.shape[0] - ROWS, TOK), F32)
         d_b[...] = d_f[...].T.astype(BF16)
 
@@ -295,48 +307,46 @@
         s_out[i - 1] = run_total(i).astype(BF16)
         cs[i] = send(s_out.at[i - 1], s_in.at[i - 1], cs_s.at[i - 1], cs_r.at[i - 1], s_dev[i])
 
-    def own_tokens(first, last):
-        def step(t, _):
-            own[t] = dot(d_t[...], tok_cols(inner(t // 2, zh, t % 2)))
+    bu, be, by = {}, {}, {}
+    factor = 1.0 / math.sqrt(16 * TOK)
+
+    def tokens_to_core():
+        for d in (1, 3, 2):
+            tx[d].wait_recv()
+        for yy in range(NY):
+            bu[yy] = send(
+                tok_in.at[2 * yy + 1 - c], tok_in_peer.at[yy], bu_s.at[yy], bu_r.at[yy], c_dev
+            )
+
+    def d_to_core(p):
+        for k in (2 * p, 2 * p + 1):
+            rows = pl.ds(*CHUNKS[k])
+            bz[k].wait_recv()
+            be[k] = send(d_in.at[rows], d_in_peer.at[rows], be_s.at[k], be_r.at[k], c_dev)
+
+    def own_tokens():
+        for k in range(NCH):
+            bd[k].wait_recv()
+        for yy in range(NY):
+            bt[yy].wait_recv()
+
+        def step(yy, _):
+            own[yy] = dot(d_t[...], tok_cols(inner(yy, zh, c))) + dot(d_peer[...], tok_peer[yy])
             return 0
 
-        lax.fori_loop(first, last, step, 0)
-
-    with jax.named_scope("token_grads_run"):
-        to_run(1)
-        own_tokens(0, 4)
-        to_run(2)
-        for d in (1, 2, 3):
-            tr[d].wait_recv()
-        pair = tok_in.at[pl.ds(2 * x, 2)]
-        for d in (1, 3, 2):
-            tx[d] = send(pair, pair, tx_s.at[d - 1], tx_r.at[d - 1], x_dev[d])
-        to_run(3)
-        own_tokens(4, 8)
-        to_run(0)
-        for i in (1, 2, 3):
-            to_strided(i)
-
-    bc, by = {}, {}
-    factor = 1.0 / math.sqrt(16 * TOK)
-
-    def whole(t, rows):
-        return own[t, rows, :] + dot(d_in[rows, :], tok_in[t])
-
-    def to_core(k):
-        rows = pl.ds(k * HALF, HALF)
-        for p in range(k, NCH, 2):
-            bz[p].wait_recv()
-        for yy in range(NY):
-            c_out[yy, rows, :] = whole(2 * yy + 1 - c, rows).astype(BF16)
-        bc[k] = send(c_out.at[:, rows], c_in.at[:, rows], bc_s.at[k], bc_r.at[k], c_dev)
+        lax.fori_loop(0, NY, step, 0)
 
     def to_y(k):
-        rows = pl.ds(k * HALF, HALF)
-        bc[k].wait_recv()
+        at, n = CHUNKS[k]
+        rows = pl.ds(at, n)
+        be[k].wait_recv()
         for d in (1, 3, 2, 0):
             yy = (y + d) % NY
-            total = whole(2 * yy + c, rows) + c_in[yy, rows, :].astype(F32)
+            total = (
+                own[yy, rows, :]
+                + dot(d_in[rows, :], tok_in[2 * yy + c])
+                + dot(d_in_peer[rows, :], tok_in_peer[yy])
+            )
             if d == 0:
                 wg_ref[rows, :] = total
                 continue
@@ -347,25 +357,37 @@
             )
 
     def finish(k):
-        rows = pl.ds(k * HALF, HALF)
+        rows = pl.ds(*CHUNKS[k])
         total = wg_ref[rows, :]
         for d in (1, 3, 2):
             by[d, k].wait_recv()
             total = total + y_in[d - 1, rows, :].astype(F32)
         wg_ref[rows, :] = total * factor
 
-    with jax.named_scope("weight_grads_first"):
-        for d in (1, 3, 2):
-            tx[d].wait_recv()
-        to_core(0)
-        to_core(1)
-        s_own[...] = run_total(0)
-
-    with jax.named_scope("weight_grads_last"):
+    with jax.named_scope("gradients"):
+        tokens_to_core()
+        d_to_core(0)
+        to_run(1)
+        own_tokens()
+        to_run(2)
+        d_to_core(1)
+        to_run(3)
+        to_run(0)
+        for yy in range(NY):
+            bu[yy].wait_recv()
         to_y(0)
         to_y(1)
-        finish(0)
-        finish(1)
+        to_strided(1)
+        to_strided(2)
+        to_y(2)
+        to_y(3)
+        to_strided(3)
+        d_to_core(2)
+        s_own[...] = run_total(0)
+        for k in range(4, NCH):
+            to_y(k)
+        for k in range(NCH):
+            finish(k)
 
     with jax.named_scope("token_grads_last"):
         for d in (1, 2, 3):
@@ -418,9 +440,11 @@
             pltpu.VMEM((64, 128), F32),
             pltpu.VMEM((NA - 1, 64, 128), BF16),
             pltpu.VMEM((NA - 1, 64, 128), BF16),
-            pltpu.VMEM((NY, ROWS, COLS), BF16),
-            pltpu.VMEM((NY, ROWS, COLS), BF16),
-            pltpu.VMEM((2 * NY, ROWS, COLS), F32),
+            pltpu.VMEM((NY, TOK, COLS), BF16),
+            pltpu.VMEM((ROWS, TOK), BF16),
+            pltpu.VMEM((NY, TOK, COLS), BF16),
+            pltpu.VMEM((ROWS, TOK), BF16),
+            pltpu.VMEM((NY, ROWS, COLS), F32),
             pltpu.VMEM((NY - 1, ROWS, COLS), BF16),
             pltpu.VMEM((NY - 1, ROWS, COLS), BF16),
             pltpu.SemaphoreType.REGULAR,
@@ -429,8 +453,11 @@
             dma((NY, 1 + NCH)), dma((NY, 1 + NCH)),
             dma((NY, 1 + NCH)), dma((NY, 1 + NCH)),
             dma((NCH,)), dma((NCH,)),
-            dma((2,)), dma((2,)),
-            dma((2, 3)), dma((2, 3)),
+            dma((NY,)), dma((NY,)),
+            dma((NCH,)), dma((NCH,)),
+            dma((NY,)), dma((NY,)),
+            dma((NCH,)), dma((NCH,)),
+            dma((NCH, 3)), dma((NCH, 3)),
             dma((4,)), dma((4,)),
             dma((2, 4)), dma((2, 4)),
             dma((4, 3)), dma((4, 3)),

time: 113 us -> 111 us (0.982); the launches traced: 112 us -> 111 us
  no operation moved by 1% of the time
where the time goes in v6:
time: 111 us
  Pallas kernels  107 us (96%)
  local copies, waits for them, and re-layouts  3.36 us (3%)
    pallas_call x1, Pallas kernels, local(): pl.pallas_call(kernel, out_shape=(jax.ShapeDtypeStruct((HALF, TOK), BF16)...  107 us
    unnamed x11, local copies, waits for them, and re-layouts  2.6 us

profile of v6, /device:TPU:1, one launch (start us, length us, event | category | flops | bytes accessed | tf_op | source)
XLA Modules:
  0.0 111.1 jit_solution(5005519425896731237)
XLA Ops:
  0.6 0.0 copy-start
  0.6 0.0 copy-start.3
  0.7 0.0 copy-start.2
  0.7 0.0 copy-start.1
  0.7 0.6 copy-done
  1.3 0.1 copy-done.3
  1.4 0.1 copy.14
  1.6 0.0 copy-done.2
  1.6 0.2 fusion
  1.9 0.1 copy-done.1
  2.0 106.8 %ffn_grads.1 = (bf16[176,128]{1,0:T(8,128)(2,1)S(1)}, f32[128,64]{1,0:T(8,128)S(1)}, f32[352,256]{1,0:T(8,128)S(1)}) custom-call(bf16[352,256]{1,0:T(8,128)(2,1)S(1)} %bitcast.12, bf16[128,4096]{1,0:T(8,128)(2,1)S(1)} %copy-done.1, bf16[176,128]{1,0:T(8,128)(2,1)S(1)} %pad.9.gh_ref), custom_call_target="tpu_custom_call" | custom-call | tf_op jit(solution)/shard_map/ffn_grads/pallas_call | solution.py:416
  108.8 0.6 slice_bitcast_fusion
  109.4 0.7 copy.13
  110.1 1.0 copy.18
  (4 shorter events, 0.0 us)
Async XLA Ops:
  0.6 0.7 copy-start
  0.6 0.8 copy-start.3
  0.7 0.9 copy-start.2
  0.7 1.3 %copy-start.1 = (bf16[128,4096]{1,0:T(8,128)(2,1)S(1)}, bf16[128,4096]{1,0:T(8,128)(2,1)}, u32[]{:S(2)}) copy-start(bf16[128,4096]{1,0:T(8,128)(2,1)} %tok_ref.1) | copy-start | bytes 3145732

commit v7 on v6

--- a/solution.py
+++ b/solution.py
@@ -170,14 +170,14 @@
         for d in (1, 2, 3):
             part = tok_in.at[shard, mine]
             ts[d] = send(part, part, ts_s.at[d - 1], ts_r.at[d - 1], s_dev[d])
+        relay(4)
+        relay(5)
+        spread(0)
+        spread(1)
         for d in range(NY):
             fc[d, 0].wait_recv()
         for at in range(0, ROWS, HALF):
             add_blocks(zh, at, HALF)
-        spread(0)
-        spread(1)
-        relay(4)
-        relay(5)
         pass_on(0)
         pass_on(1)
         spread(2)
@@ -365,24 +365,24 @@
         wg_ref[rows, :] = total * factor
 
     with jax.named_scope("gradients"):
+        to_run(1)
         tokens_to_core()
-        d_to_core(0)
-        to_run(1)
         own_tokens()
         to_run(2)
-        d_to_core(1)
+        d_to_core(0)
         to_run(3)
         to_run(0)
         for yy in range(NY):
             bu[yy].wait_recv()
         to_y(0)
-        to_y(1)
         to_strided(1)
         to_strided(2)
+        to_y(1)
+        d_to_core(1)
+        to_strided(3)
+        d_to_core(2)
         to_y(2)
         to_y(3)
-        to_strided(3)
-        d_to_core(2)
         s_own[...] = run_total(0)
         for k in range(4, NCH):
             to_y(k)

time: 111 us -> 114 us (1.027)
  Pallas kernels: 107 us -> 109 us
    pallas_call x1, Pallas kernels: 107 us -> 109 us  [local(): pl.pallas_call(kernel, out_shape=(jax.ShapeDtypeStruct((HALF, TOK), BF16)...]
where the time goes in v7:
time: 114 us
  Pallas kernels  109 us (96%)
  local copies, waits for them, and re-layouts  3.36 us (3%)
    pallas_call x1, Pallas kernels, local(): pl.pallas_call(kernel, out_shape=(jax.ShapeDtypeStruct((HALF, TOK), BF16)...  109 us
    unnamed x11, local copies, waits for them, and re-layouts  2.6 us

profile of v7, /device:TPU:1, one launch (start us, length us, event | category | flops | bytes accessed | tf_op | source)
XLA Modules:
  0.0 113.7 jit_solution(7075093852739973406)
XLA Ops:
  0.6 0.0 copy-start
  0.6 0.0 copy-start.3
  0.7 0.0 copy-start.2
  0.7 0.0 copy-start.1
  0.7 0.6 copy-done
  1.3 0.1 copy-done.3
  1.4 0.1 copy.14
  1.6 0.0 copy-done.2
  1.6 0.2 fusion
  1.9 0.1 copy-done.1
  2.0 109.3 %ffn_grads.1 = (bf16[176,128]{1,0:T(8,128)(2,1)S(1)}, f32[128,64]{1,0:T(8,128)S(1)}, f32[352,256]{1,0:T(8,128)S(1)}) custom-call(bf16[352,256]{1,0:T(8,128)(2,1)S(1)} %bitcast.12, bf16[128,4096]{1,0:T(8,128)(2,1)S(1)} %copy-done.1, bf16[176,128]{1,0:T(8,128)(2,1)S(1)} %pad.9.gh_ref), custom_call_target="tpu_custom_call" | custom-call | tf_op jit(solution)/shard_map/ffn_grads/pallas_call | solution.py:416
  111.4 0.6 slice_bitcast_fusion
  112.0 0.7 copy.13
  112.7 1.0 copy.18
  (4 shorter events, 0.0 us)
Async XLA Ops:
  0.6 0.7 copy-start
  0.6 0.8 copy-start.3
  0.7 0.9 copy-start.2
  0.7 1.3 %copy-start.1 = (bf16[128,4096]{1,0:T(8,128)(2,1)S(1)}, bf16[128,4096]{1,0:T(8,128)(2,1)}, u32[]{:S(2)}) copy-start(bf16[128,4096]{1,0:T(8,128)(2,1)} %tok_ref.1) | copy-start | bytes 3145732

commit v8 on v7

--- a/solution.py
+++ b/solution.py
@@ -170,14 +170,14 @@
         for d in (1, 2, 3):
             part = tok_in.at[shard, mine]
             ts[d] = send(part, part, ts_s.at[d - 1], ts_r.at[d - 1], s_dev[d])
-        relay(4)
-        relay(5)
-        spread(0)
-        spread(1)
         for d in range(NY):
             fc[d, 0].wait_recv()
         for at in range(0, ROWS, HALF):
             add_blocks(zh, at, HALF)
+        spread(0)
+        spread(1)
+        relay(4)
+        relay(5)
         pass_on(0)
         pass_on(1)
         spread(2)

time: 114 us -> 113 us (level)
  no operation moved by 1% of the time
where the time goes in v8:
time: 113 us
  Pallas kernels  109 us (96%)
  local copies, waits for them, and re-layouts  3.36 us (3%)
    pallas_call x1, Pallas kernels, local(): pl.pallas_call(kernel, out_shape=(jax.ShapeDtypeStruct((HALF, TOK), BF16)...  109 us
    unnamed x11, local copies, waits for them, and re-layouts  2.6 us

profile of v8, /device:TPU:1, one launch (start us, length us, event | category | flops | bytes accessed | tf_op | source)
XLA Modules:
  0.0 113.1 jit_solution(873865709367646989)
XLA Ops:
  0.6 0.0 copy-start
  0.6 0.0 copy-start.3
  0.7 0.0 copy-start.2
  0.7 0.0 copy-start.1
  0.7 0.6 copy-done
  1.3 0.1 copy-done.3
  1.4 0.1 copy.14
  1.6 0.0 copy-done.2
  1.6 0.2 fusion
  1.9 0.1 copy-done.1
  2.0 108.8 %ffn_grads.1 = (bf16[176,128]{1,0:T(8,128)(2,1)S(1)}, f32[128,64]{1,0:T(8,128)S(1)}, f32[352,256]{1,0:T(8,128)S(1)}) custom-call(bf16[352,256]{1,0:T(8,128)(2,1)S(1)} %bitcast.12, bf16[128,4096]{1,0:T(8,128)(2,1)S(1)} %copy-done.1, bf16[176,128]{1,0:T(8,128)(2,1)S(1)} %pad.9.gh_ref), custom_call_target="tpu_custom_call" | custom-call | tf_op jit(solution)/shard_map/ffn_grads/pallas_call | solution.py:416
  110.8 0.6 slice_bitcast_fusion
  111.4 0.7 copy.13
  112.1 1.0 copy.18
  (4 shorter events, 0.0 us)
Async XLA Ops:
  0.6 0.7 copy-start
  0.6 0.8 copy-start.3
  0.7 0.9 copy-start.2
  0.7 1.3 %copy-start.1 = (bf16[128,4096]{1,0:T(8,128)(2,1)S(1)}, bf16[128,4096]{1,0:T(8,128)(2,1)}, u32[]{:S(2)}) copy-start(bf16[128,4096]{1,0:T(8,128)(2,1)} %tok_ref.1) | copy-start | bytes 3145732

commit v9 on v6

--- a/solution.py
+++ b/solution.py
@@ -17,7 +17,7 @@
 ROWS = 2 * HALF
 COLS = 256
 TOK = 128
-CHUNKS = ((0, 80), (176, 80), (80, 64), (256, 64), (144, 32), (320, 32))
+CHUNKS = ((0, 96), (176, 96), (96, 48), (272, 48), (144, 32), (320, 32))
 NCH = len(CHUNKS)
 
 

time: 111 us -> 114 us (1.027)
  Pallas kernels: 107 us -> 109 us
    pallas_call x1, Pallas kernels: 107 us -> 109 us  [local(): pl.pallas_call(kernel, out_shape=(jax.ShapeDtypeStruct((HALF, TOK), BF16)...]
where the time goes in v9:
time: 114 us
  Pallas kernels  109 us (96%)
  local copies, waits for them, and re-layouts  3.36 us (3%)
    pallas_call x1, Pallas kernels, local(): pl.pallas_call(kernel, out_shape=(jax.ShapeDtypeStruct((HALF, TOK), BF16)...  109 us
    unnamed x11, local copies, waits for them, and re-layouts  2.6 us

profile of v9, /device:TPU:1, one launch (start us, length us, event | category | flops | bytes accessed | tf_op | source)
XLA Modules:
  0.0 113.6 jit_solution(16024673365365720076)
XLA Ops:
  0.6 0.0 copy-start
  0.6 0.0 copy-start.3
  0.7 0.0 copy-start.2
  0.7 0.0 copy-start.1
  0.7 0.6 copy-done
  1.3 0.1 copy-done.3
  1.4 0.1 copy.14
  1.6 0.0 copy-done.2
  1.6 0.2 fusion
  1.9 0.1 copy-done.1
  2.0 109.3 %ffn_grads.1 = (bf16[176,128]{1,0:T(8,128)(2,1)S(1)}, f32[128,64]{1,0:T(8,128)S(1)}, f32[352,256]{1,0:T(8,128)S(1)}) custom-call(bf16[352,256]{1,0:T(8,128)(2,1)S(1)} %bitcast.12, bf16[128,4096]{1,0:T(8,128)(2,1)S(1)} %copy-done.1, bf16[176,128]{1,0:T(8,128)(2,1)S(1)} %pad.9.gh_ref), custom_call_target="tpu_custom_call" | custom-call | tf_op jit(solution)/shard_map/ffn_grads/pallas_call | solution.py:416
  111.3 0.6 slice_bitcast_fusion
  111.9 0.7 copy.13
  112.6 1.0 copy.18
  (4 shorter events, 0.0 us)
Async XLA Ops:
  0.6 0.7 copy-start
  0.6 0.8 copy-start.3
  0.7 0.9 copy-start.2
  0.7 1.3 %copy-start.1 = (bf16[128,4096]{1,0:T(8,128)(2,1)S(1)}, bf16[128,4096]{1,0:T(8,128)(2,1)}, u32[]{:S(2)}) copy-start(bf16[128,4096]{1,0:T(8,128)(2,1)} %tok_ref.1) | copy-start | bytes 3145732
